TPU v7x, 128 devices: a whole 4x4x4 slice. The times are simulated.
128 devices in a mesh: row: 8 (over x, core), col: 16 (over y, z).
Axes of the slice: x: 4, y: 4, z: 4, core: 2. Of those that a mesh axis runs over, the one named last changes fastest.
Arguments:
- theta: bfloat16 [8192, 4, 4, 2048], P('row', None, None, 'col'), may hold values from -6 to 6
- gate: bfloat16 [4, 4, 4, 4], replicated, may hold values from -1.5 to 1.5
- warm_start: bfloat16 [16, 4, 2048, 512], P('row', None, 'col'), may hold values from -0.0625 to 0.0625
- slot_sector: int32 [16], replicated, may hold values from 0 to 15, each once
- kept: int32 [16], replicated, may hold values from 128 to 512
- block_offsets: int32 [8, 16], replicated, may hold values from 0 to 992, as said below
Outputs:
- left_factor: float32 [768, 16, 4, 512], P('col', 'row')
- right_factor: float32 [16, 4, 2048, 512], P('row', None, 'col')
Inputs may be any that keep to these rules, and one draw needn't show every extreme that they name: `block_offsets`: each device's block lists the sectors in order; every sector has 32 to 96 states in every block, both ends reached; offsets start at 0 and the counts of a block add up to 1024.
All inputs are finite; a program needn't handle non-finite values.
Results may differ from a plain program's by a relative error of at most 0.0042.
Values may be sent and summed in bfloat16 or wider, within the bound.
A program may use at most 512 MiB of HBM per device.

v0:
```python
import jax
import jax.numpy as jnp
from jax import lax
from jax.sharding import PartitionSpec as P

NMAX = 96


damping = 0.25


def refine_step(gram_matrix, correlation, kept_rank):
    kept_most = gram_matrix.shape[0]
    identity = jnp.eye(kept_most, dtype=jnp.float32)
    lambdas = jnp.diagonal(gram_matrix) / (jnp.diagonal(correlation) + 1e-06)
    resid = identity - correlation
    differ = lambdas[None, :] - lambdas[:, None]
    divisor = differ * differ + (damping * (lambdas[:, None] + lambdas[None, :])) ** 2 + 1e-06
    offdiag = (gram_matrix + lambdas[None, :] * resid) * differ / divisor
    indices = jnp.arange(kept_most)
    inside = (indices[:, None] < kept_rank) & (indices[None, :] < kept_rank)
    result = jnp.where(identity > 0.5, 0.5 * resid, offdiag)
    return jnp.where(inside, result, jnp.float32(0.0))


def shards(theta, gate, warm_start, slot_sector, kept, block_offsets):
    row_devices = lax.axis_size("row")
    my_row = lax.axis_index("row")
    block_rows = theta.shape[0]
    bond_cols = theta.shape[3]
    sectors = slot_sector.shape[0]
    per_group = sectors // row_devices
    kept_most = warm_start.shape[3]
    gated = jnp.einsum("abef,refc->rabc", gate, theta, preferred_element_type=jnp.float32)
    gated = gated.astype(jnp.bfloat16).reshape(block_rows, 4, 4 * bond_cols)
    closing = jnp.full((row_devices, 1), block_rows, jnp.int32)
    counts = jnp.concatenate([block_offsets[:, 1:], closing], axis=1) - block_offsets
    mine_start = lax.dynamic_index_in_dim(block_offsets, my_row, 0, keepdims=False)
    mine_count = lax.dynamic_index_in_dim(counts, my_row, 0, keepdims=False)
    sector_ids = jnp.arange(sectors, dtype=jnp.int32)
    chooser = (slot_sector[:, None] == sector_ids[None, :]).astype(jnp.int32)
    slot_start = jnp.sum(chooser * mine_start[None, :], axis=1)
    slot_count = jnp.sum(chooser * mine_count[None, :], axis=1)
    places = jnp.arange(NMAX, dtype=jnp.int32)
    row_index = jnp.minimum(slot_start[None, :] + places[:, None], block_rows - 1)
    live_mask = places[:, None] < slot_count[None, :]
    outgoing = jnp.where(live_mask[:, :, None, None], gated[row_index], jnp.zeros((), jnp.bfloat16))
    blocks = lax.all_to_all(outgoing, "row", split_axis=1, concat_axis=0, tiled=True)
    vectors = warm_start.reshape(per_group, 4 * bond_cols, kept_most)
    my_sectors = lax.dynamic_slice_in_dim(slot_sector, my_row * per_group, per_group, 0)
    my_chooser = (my_sectors[:, None] == sector_ids[None, :]).astype(jnp.int32)
    my_kept = jnp.sum(my_chooser * kept[None, :], axis=1)
    correlation_part = jnp.einsum(
        "snk,snl->skl", vectors, vectors, preferred_element_type=jnp.float32
    )
    projected = lax.psum_scatter(
        jnp.einsum("istn,snk->istk", blocks, vectors, preferred_element_type=jnp.float32),
        "col",
        scatter_dimension=0,
        tiled=True,
    )
    projected_b = projected.astype(jnp.bfloat16)
    gram_part = jnp.einsum(
        "istk,istl->skl", projected_b, projected_b, preferred_element_type=jnp.float32
    )
    gram_matrix, correlation = lax.psum((gram_part, correlation_part), "col")
    corr_b = jax.vmap(refine_step)(gram_matrix, correlation, my_kept).astype(jnp.bfloat16)
    kept_mask = (jnp.arange(kept_most)[None, :] < my_kept[:, None]).astype(jnp.float32)
    new_vectors = vectors.astype(jnp.float32) + jnp.einsum(
        "snk,skl->snl", vectors, corr_b, preferred_element_type=jnp.float32
    )
    new_vectors = new_vectors * kept_mask[:, None, :]
    left = projected + jnp.einsum(
        "istk,skl->istl", projected_b, corr_b, preferred_element_type=jnp.float32
    )
    left = left * kept_mask[None, :, None, :]
    return (left, new_vectors.reshape(per_group, 4, bond_cols, kept_most))


def solution(mesh):
    in_specs = (P("row", None, None, "col"), P(), P("row", None, "col", None), P(), P(), P())
    out_specs = (P("col", "row", None, None), P("row", None, "col", None))
    return jax.shard_map(shards, mesh=mesh, in_specs=in_specs, out_specs=out_specs, check_vma=False)
```

profile of v0, /device:TPU:1, one launch (start us, length us, event | category | flops | bytes accessed | tf_op | source)
XLA Modules:
  0.0 485.5 jit_solution(11147992323362789733)
XLA Ops:
  7.2 0.8 slice.3
  9.4 0.8 select_reduce_fusion.1
  10.3 6.1 %fusion.1 = bf16[1024,4,4,128]{3,2,1,0:T(4,128)(2,1)} fusion(bf16[1024,4,4,128]{3,2,1,0:T(4,128)(2,1)} %param.6, bf16[4,4,4,4]{3,2,1,0:T(4,128)(2,1)} %param.7), kind=kOutput, calls=%fused_computation.7 | convolution fusion | flops 69206016 | bytes 8389120 | tf_op jit(solution)/shard_map/abef,refc->rabc/dot_general | solution.py:34
  16.5 7.2 %reshape.172 = bf16[1024,4,512]{2,1,0:T(4,128)(2,1)} reshape(bf16[1024,4,4,128]{3,2,1,0:T(4,128)(2,1)} %fusion.1) | data formatting | bytes 8388608 | tf_op jit(solution)/shard_map/reshape | solution.py:35
  23.7 10.8 %gather_fusion = bf16[1536,4,512]{2,1,0:T(4,128)(2,1)} fusion(bf16[1024,4,512]{2,1,0:T(4,128)(2,1)} %reshape.172, s32[2048]{0:T(1024)S(1)} %pad_clamp_fusion), kind=kCustom, calls=%fused_computation | custom fusion | bytes 12589056 | tf_op jit(solution)/shard_map/gather | solution.py:47
  34.5 4.0 copy.53
  39.1 3.6 copy.54
  42.6 77.7 %all_to_all.18 = bf16[96,16,4,512]{3,0,2,1:T(8,128)(2,1)S(1)} all-to-all(bf16[96,16,4,512]{3,0,2,1:T(8,128)(2,1)S(1)} %copy.54), channel_id=1, replica_groups=mesh['row'=8,'col'=16] {'row'}, dimensions={1} | all-to-all | bytes 12582912 | tf_op jit(solution)/shard_map/all_to_all | solution.py:48
  120.4 0.7 copy.55
  121.6 6.4 %convolution_bitcast_fusion = f32[768,2,4,512]{3,0,2,1:T(8,128)} fusion(bf16[768,2,4,512]{3,0,2,1:T(8,128)(2,1)S(1)} %bitcast.65, bf16[2,512,512,1]{2,1,3,0:T(8,128)(2,1)S(1)} %bitcast.68), kind=kOutput, calls=%fused_computation.5 | convolution fusion | flops 3221225472 | bytes 19922944 | tf_op jit(solution)/shard_map/istn,snk->istk/dot_general | solution.py:57
  128.0 2.1 fusion.21
  130.1 93.3 %reduce-scatter.2.cloned.1.call-done = f32[48,2,4,512]{3,0,2,1:T(8,128)} async-done(((f32[768,2,4,512]{3,0,2,1:T(8,128)}), f32[48,2,4,512]{3,0,2,1:T(8,128)}) %reduce-scatter.2.cloned.1.call-update) | async-done | bytes 786448 | tf_op jit(solution)/shard_map/reduce_scatter | solution.py:56
  223.4 3.3 convolution_bitcast_fusion.1
  227.7 1.2 fusion.14
  228.9 101.3 %all-reduce.4.cloned.1.call-done = (f32[2,512,512]{2,1,0:T(8,128)}, f32[2,512,512]{2,1,0:T(8,128)}) async-done(((f32[2,512,512]{2,1,0:T(8,128)}, f32[2,512,512]{2,1,0:T(8,128)}), (f32[2,512,512]{2,1,0:T(8,128)}, f32[2,512,512]{2,1,0:T(8,128)})) %all-reduce.4.cloned.1.call-update) | async-done | bytes 4194320 | tf_op jit(solution)/shard_map/psum | solution.py:66
  330.2 61.4 %copy.57 = f32[2,512,512]{0,2,1:T(8,128)} copy(f32[2,512,512]{2,1,0:T(8,128)} %get-tuple-element.16) | data formatting | bytes 4194304 | tf_op jit(solution)/shard_map/psum | solution.py:66
  391.6 61.6 %copy.58 = f32[2,512,512]{0,2,1:T(8,128)} copy(f32[2,512,512]{2,1,0:T(8,128)} %get-tuple-element.17) | data formatting | bytes 4194304 | tf_op jit(solution)/shard_map/psum | solution.py:66
  453.2 8.0 %gather_fusion.1 = f32[512,2]{1,0:T(8,128)} fusion(f32[2,512,512]{0,2,1:T(8,128)} %copy.57, s32[512]{0:T(512)S(1)} %bitcast.63), kind=kCustom, calls=%fused_computation.1 | custom fusion | bytes 12288 | tf_op jit(solution)/shard_map/vmap(jit(diagonal))/cond/branch_0_fun/gather | solution.py:15
  461.1 8.0 %gather_fusion.2 = f32[512,2]{1,0:T(8,128)} fusion(f32[2,512,512]{0,2,1:T(8,128)} %copy.58, s32[512]{0:T(512)S(1)} %bitcast.64), kind=kCustom, calls=%fused_computation.2 | custom fusion | bytes 12288 | tf_op jit(solution)/shard_map/vmap(jit(diagonal))/cond/branch_0_fun/gather | solution.py:15
  469.1 1.8 divide_bitcast_fusion
  470.9 1.1 copy.59
  471.9 2.9 fusion.10
  474.8 2.0 fusion.9
  477.3 1.4 copy.61
  (26 shorter events, 4.0 us)
Async XLA Ops:
  7.2 216.3 %reduce-scatter.2.cloned.1.call-start = ((), (), s32[]{:S(2)}) async-start(), calls=%async_computation.2 | async-start | bytes 13369344 | tf_op jit(solution)/shard_map/reduce_scatter | solution.py:56
  120.4 1.2 copy-start
  128.0 202.2 %all-reduce.4.cloned.1.call-start = ((), (), s32[]{:S(2)}) async-start(), calls=%async_computation.3 | async-start | bytes 8388608 | tf_op jit(solution)/shard_map/psum | solution.py:66
  226.8 0.7 copy-start.3
  226.8 0.7 copy-start.4
  391.6 80.3 %copy-start.1 = (f32[2,512,512]{2,1,0:T(8,128)S(1)}, f32[2,512,512]{2,1,0:T(8,128)}, u32[]{:S(2)}) copy-start(f32[2,512,512]{2,1,0:T(8,128)} %get-tuple-element.16) | copy-start | bytes 6291460
  474.8 2.1 copy-start.2
Sparse Core Ops, SparseCore 0:
  128.1 95.3 reduce-scatter.1
  227.5 102.6 all-reduce.3
where the time goes:
time: 490 us; the launch traced here: 485 us
  waiting for transfers between devices  195 us (40%)
  local copies, waits for them, and re-layouts  170 us (35%)
  blocking collectives  77.7 us (16%)
  matrix products  20.3 us (4%)
  between operations  14.1 us (3%)
  other arithmetic  8.18 us (2%)
    psum x2, local copies, waits for them, and re-layouts, shards(): gram_matrix, correlation = lax.psum((gram_part, correlation_part), 'col')  123 us
    psum x1, waiting for transfers between devices, shards(): gram_matrix, correlation = lax.psum((gram_part, correlation_part), 'col')  101 us
    reduce_scatter x1, waiting for transfers between devices, shards(): lax.psum_scatter(jnp.einsum('istn,snk->istk', blocks, vectors, preferred_...  93.3 us
    all_to_all x1, blocking collectives, shards(): lax.all_to_all(outgoing, 'row', split_axis=1, concat_axis=0, tiled=True)  77.7 us
    gather x2, local copies, waits for them, and re-layouts, refine_step(): lambdas = jnp.diagonal(gram_matrix) / (jnp.diagonal(correlation) + 1e-06)  15.9 us
    gather x2, local copies, waits for them, and re-layouts, shards(): gated[row_index]  14.8 us
  transfers between devices with their start and end apart: 2, of which 2 were waited for; matrix products, arithmetic and copies ran while one was open for 1% of the time, Pallas kernels for 0%

commit v1 on v0

--- a/solution.py
+++ b/solution.py
@@ -9,10 +9,10 @@
 damping = 0.25
 
 
-def refine_step(gram_matrix, correlation, kept_rank):
+def refine_step(gram_matrix, correlation, gram_diag, corr_diag, kept_rank):
     kept_most = gram_matrix.shape[0]
     identity = jnp.eye(kept_most, dtype=jnp.float32)
-    lambdas = jnp.diagonal(gram_matrix) / (jnp.diagonal(correlation) + 1e-06)
+    lambdas = gram_diag / (corr_diag + 1e-06)
     resid = identity - correlation
     differ = lambdas[None, :] - lambdas[:, None]
     divisor = differ * differ + (damping * (lambdas[:, None] + lambdas[None, :])) ** 2 + 1e-06
@@ -53,6 +53,8 @@
     correlation_part = jnp.einsum(
         "snk,snl->skl", vectors, vectors, preferred_element_type=jnp.float32
     )
+    correlation = lax.psum(correlation_part, "col")
+    identity = jnp.eye(kept_most, dtype=jnp.float32)[None]
     projected = lax.psum_scatter(
         jnp.einsum("istn,snk->istk", blocks, vectors, preferred_element_type=jnp.float32),
         "col",
@@ -63,8 +65,10 @@
     gram_part = jnp.einsum(
         "istk,istl->skl", projected_b, projected_b, preferred_element_type=jnp.float32
     )
-    gram_matrix, correlation = lax.psum((gram_part, correlation_part), "col")
-    corr_b = jax.vmap(refine_step)(gram_matrix, correlation, my_kept).astype(jnp.bfloat16)
+    gram_matrix = lax.psum(gram_part, "col")
+    gram_diag = jnp.sum(gram_matrix * identity, axis=1)
+    corr_diag = jnp.sum(correlation * identity, axis=1)
+    corr_b = jax.vmap(refine_step)(gram_matrix, correlation, gram_diag, corr_diag, my_kept).astype(jnp.bfloat16)
     kept_mask = (jnp.arange(kept_most)[None, :] < my_kept[:, None]).astype(jnp.float32)
     new_vectors = vectors.astype(jnp.float32) + jnp.einsum(
         "snk,skl->snl", vectors, corr_b, preferred_element_type=jnp.float32

time: 490 us -> 347 us (0.71)
  local copies, waits for them, and re-layouts: 170 us -> 30.9 us
    psum x2 -> x0, local copies, waits for them, and re-layouts: 123 us -> none  [shards(): gram_matrix, correlation = lax.psum((gram_part, correlation_part), 'col')]
    gather x2 -> x0, local copies, waits for them, and re-layouts: 15.9 us -> none  [refine_step(): lambdas = jnp.diagonal(gram_matrix) / (jnp.diagonal(correlation) + 1e-06)]
where the time goes in v1:
time: 347 us; the launch traced here: 346 us
  waiting for transfers between devices  196 us (56%)
  blocking collectives  77.7 us (22%)
  local copies, waits for them, and re-layouts  30.9 us (9%)
  matrix products  20.2 us (6%)
  between operations  14.2 us (4%)
  other arithmetic  7.09 us (2%)
    psum x1, waiting for transfers between devices, shards(): gram_matrix = lax.psum(gram_part, 'col')  102 us
    reduce_scatter x1, waiting for transfers between devices, shards(): lax.psum_scatter(jnp.einsum('istn,snk->istk', blocks, vectors, preferred_...  93.4 us
    all_to_all x1, blocking collectives, shards(): lax.all_to_all(outgoing, 'row', split_axis=1, concat_axis=0, tiled=True)  77.7 us
    gather x2, local copies, waits for them, and re-layouts, shards(): gated[row_index]  14.9 us
    reshape x1, local copies, waits for them, and re-layouts, shards(): gated = gated.astype(jnp.bfloat16).reshape(block_rows, 4, 4 * bond_cols)  7.22 us
  transfers between devices with their start and end apart: 2, of which 2 were waited for; matrix products, arithmetic and copies ran while one was open for 1% of the time, Pallas kernels for 0%

profile of v1, /device:TPU:1, one launch (start us, length us, event | category | flops | bytes accessed | tf_op | source)
XLA Modules:
  0.0 346.0 jit_solution(13557747863219205572)
XLA Ops:
  7.2 0.8 slice.3
  8.0 0.7 pad_subtract_fusion
  8.7 0.7 dynamic-slice_bitcast_fusion
  9.4 0.8 select_reduce_fusion.1
  10.3 6.1 %fusion.1 = bf16[1024,4,4,128]{3,2,1,0:T(4,128)(2,1)} fusion(bf16[1024,4,4,128]{3,2,1,0:T(4,128)(2,1)} %param.6, bf16[4,4,4,4]{3,2,1,0:T(4,128)(2,1)} %param.7), kind=kOutput, calls=%fused_computation.5 | convolution fusion | flops 69206016 | bytes 8389120 | tf_op jit(solution)/shard_map/abef,refc->rabc/dot_general | solution.py:34
  16.4 7.2 %reshape.172 = bf16[1024,4,512]{2,1,0:T(4,128)(2,1)} reshape(bf16[1024,4,4,128]{3,2,1,0:T(4,128)(2,1)} %fusion.1) | data formatting | bytes 8388608 | tf_op jit(solution)/shard_map/reshape | solution.py:35
  23.7 10.8 %gather_fusion = bf16[1536,4,512]{2,1,0:T(4,128)(2,1)} fusion(bf16[1024,4,512]{2,1,0:T(4,128)(2,1)} %reshape.172, s32[2048]{0:T(1024)S(1)} %pad_clamp_fusion), kind=kCustom, calls=%fused_computation | custom fusion | bytes 12589056 | tf_op jit(solution)/shard_map/gather | solution.py:47
  34.5 4.0 %copy.33 = bf16[1536,4,512]{2,0,1:T(8,128)(2,1)S(1)} copy(bf16[1536,4,512]{2,1,0:T(4,128)(2,1)} %gather_fusion) | data formatting | bytes 12582912 | tf_op jit(solution)/shard_map/gather | solution.py:47
  38.5 0.5 broadcast_select_fusion
  39.1 3.6 %copy.34 = bf16[96,16,4,512]{3,0,2,1:T(8,128)(2,1)S(1)} copy(bf16[96,16,4,512]{3,1,0,2:T(8,128)(2,1)S(1)} %broadcast_select_fusion) | data formatting | bytes 12582912 | tf_op jit(solution)/shard_map/jit(_where)/select_n | solution.py:47
  42.7 77.7 %all_to_all.18 = bf16[96,16,4,512]{3,0,2,1:T(8,128)(2,1)S(1)} all-to-all(bf16[96,16,4,512]{3,0,2,1:T(8,128)(2,1)S(1)} %copy.34), channel_id=1, replica_groups=mesh['row'=8,'col'=16] {'row'}, dimensions={1} | all-to-all | bytes 12582912 | tf_op jit(solution)/shard_map/all_to_all | solution.py:48
  120.4 0.7 copy.35
  121.1 0.5 copy-done
  121.6 6.4 %convolution_bitcast_fusion = f32[768,2,4,512]{3,0,2,1:T(8,128)} fusion(bf16[768,2,4,512]{3,0,2,1:T(8,128)(2,1)S(1)} %bitcast.60, bf16[2,512,512,1]{2,1,3,0:T(8,128)(2,1)S(1)} %bitcast.63), kind=kOutput, calls=%fused_computation.3 | convolution fusion | flops 3221225472 | bytes 19922944 | tf_op jit(solution)/shard_map/istn,snk->istk/dot_general | solution.py:59
  128.0 2.1 fusion.21
  130.2 93.4 %reduce-scatter.2.cloned.1.call-done = f32[48,2,4,512]{3,0,2,1:T(8,128)} async-done(((f32[768,2,4,512]{3,0,2,1:T(8,128)}), f32[48,2,4,512]{3,0,2,1:T(8,128)}) %reduce-scatter.2.cloned.1.call-update) | async-done | bytes 786448 | tf_op jit(solution)/shard_map/reduce_scatter | solution.py:58
  223.6 3.2 convolution_bitcast_fusion.1
  226.8 0.6 copy-done.4
  228.0 102.3 %all-reduce.4.cloned.1.call-done = (f32[2,512,512]{2,1,0:T(8,128)}, f32[2,512,512]{2,1,0:T(8,128)}) async-done(((f32[2,512,512]{2,1,0:T(8,128)}, f32[2,512,512]{2,1,0:T(8,128)}), (f32[2,512,512]{2,1,0:T(8,128)}, f32[2,512,512]{2,1,0:T(8,128)})) %all-reduce.4.cloned.1.call-update) | async-done | bytes 4194320 | tf_op jit(solution)/shard_map/psum | solution.py:68
  330.3 3.0 multiply_reduce_fusion
  333.4 0.4 copy-done.2
  333.8 1.5 fusion.10
  335.3 2.0 fusion.9
  337.7 1.4 copy.37
  (23 shorter events, 1.2 us)
Async XLA Ops:
  7.2 216.4 %reduce-scatter.2.cloned.1.call-start = ((), (), s32[]{:S(2)}) async-start(), calls=%async_computation.2 | async-start | bytes 13369344 | tf_op jit(solution)/shard_map/reduce_scatter | solution.py:58
  120.4 1.2 copy-start
  128.0 202.3 %all-reduce.4.cloned.1.call-start = ((), (), s32[]{:S(2)}) async-start(), calls=%async_computation.3 | async-start | bytes 8388608 | tf_op jit(solution)/shard_map/psum | solution.py:68
  226.8 0.7 copy-start.4
  226.8 0.7 copy-start.5
  330.3 3.1 copy-start.1
  330.3 3.5 %copy-start.2 = (f32[2,512,512]{2,1,0:T(8,128)S(1)}, f32[2,512,512]{2,1,0:T(8,128)}, u32[]{:S(2)}) copy-start(f32[2,512,512]{2,1,0:T(8,128)} %get-tuple-element.19) | copy-start | bytes 6291460
  335.3 2.1 copy-start.3
Sparse Core Ops, SparseCore 0:
  128.1 95.4 reduce-scatter.1
  227.6 102.6 all-reduce.3

commit v2 on v1

v2 whole, which is shorter than its diff:
```python
import functools

import jax
import jax.numpy as jnp
from jax import lax
from jax.experimental import pallas as pl
from jax.experimental.pallas import tpu as pltpu
from jax.sharding import PartitionSpec as P

NMAX = 96
HALF = NMAX // 2
SITES = 4
LANES = 128
KEPT = 512
ROWS = 1024
DAMPING = 0.25
MESH = pl.DeviceIdType.MESH

ORDER = (
    (0, 0), (0, 1), (1, 0), (1, 1),
    (2, 0), (3, 0), (4, 0), (5, 0),
    (2, 1), (3, 1), (4, 1), (5, 1),
    (6, 0), (6, 1), (7, 0), (7, 1),
)
UNITS = len(ORDER)
LAG = (2, 4, 6)


def project_kernel(
    theta_ref, gate_ref, v_ref, sector_ref, offset_ref, fin_ref,
    th, bd, ap, vall, part, half_in, ring_in, quart, quart_in, done,
    th_sem, v_sem, v_send, v_recv, half_send, half_recv, ring_send, ring_recv,
    quart_send, quart_recv, fin_send, fin_recv,
):
    row, col = lax.axis_index("row"), lax.axis_index("col")
    x, core = row // 2, row % 2
    y, z = col // 4, col % 4
    other = 1 - core

    def rows_at(step, which):
        return ((x + step) % 4) * 2 + which

    places = (
        row, rows_at(0, other), rows_at(3, core), rows_at(1, core),
        rows_at(3, other), rows_at(1, other), rows_at(2, core), rows_at(2, other),
    )
    sibling, before, after = places[1], places[2], places[3]

    def along(axis, step):
        if axis == 0:
            return {"row": row, "col": y * 4 + (z + step) % 4}
        return {"row": row, "col": ((y + step) % 4) * 4 + z}

    sends = []

    def send(src, dst, send_sem, recv_sem, where):
        copy = pltpu.make_async_remote_copy(
            src_ref=src, dst_ref=dst, send_sem=send_sem, recv_sem=recv_sem,
            device_id=where, device_id_type=MESH,
        )
        copy.start()
        sends.append(copy)

    def arrived(dst, sem):
        pltpu.make_async_copy(dst, dst, sem).wait()

    theta_in = pltpu.make_async_copy(theta_ref, th.at[pl.ds(0, ROWS)], th_sem)
    theta_in.start()
    v_in = pltpu.make_async_copy(v_ref, vall.at[0], v_sem)
    v_in.start()
    for s in range(2):
        for n, (where, place) in enumerate(((sibling, 1), (after, 2), (before, 3))):
            send(v_ref.at[s], vall.at[place, s], v_send.at[3 * s + n], v_recv.at[place, s], {"row": where, "col": col})

    big_r = lax.broadcasted_iota(jnp.int32, (256, 256), 0)
    big_c = lax.broadcasted_iota(jnp.int32, (256, 256), 1)
    left_hot = (lax.broadcasted_iota(jnp.int32, (256, 16), 0) // 16 == lax.broadcasted_iota(jnp.int32, (256, 16), 1))
    right_hot = (lax.broadcasted_iota(jnp.int32, (16, 256), 1) % 16 == lax.broadcasted_iota(jnp.int32, (16, 256), 0))
    spread = jnp.dot(left_hot.astype(jnp.bfloat16), gate_ref[...], preferred_element_type=jnp.float32)
    spread = jnp.dot(spread.astype(jnp.bfloat16), right_hot.astype(jnp.bfloat16), preferred_element_type=jnp.float32)
    bd[...] = jnp.where(big_r % 16 == big_c // 16, spread, 0.0).astype(jnp.bfloat16)
    th[pl.ds(ROWS, NMAX)] = jnp.zeros((NMAX, 16, LANES), jnp.bfloat16)
    theta_in.wait()
    v_in.wait()

    state = lax.broadcasted_iota(jnp.int32, (256, 256), 0) % 16
    state = state + 16 * (lax.broadcasted_iota(jnp.int32, (256, 256), 1) // LANES)

    def compute(u):
        place, s = ORDER[u]
        slot = places[place] * 2 + s
        if place:
            arrived(vall.at[place, s], v_recv.at[place, s])
            if place in (2, 3, 6):
                share = {2: 4, 3: 5, 6: 7}[place]
                if place == 2 and s == 0:
                    send(vall.at[2, 0], vall.at[6, 0], v_send.at[6], v_recv.at[6, 0], {"row": after, "col": col})
                if place == 3 and s == 1:
                    send(vall.at[3, 1], vall.at[6, 1], v_send.at[7], v_recv.at[6, 1], {"row": before, "col": col})
                n = 8 + 2 * (2, 3, 6).index(place) + s
                send(vall.at[place, s], vall.at[share, s], v_send.at[n], v_recv.at[share, s], {"row": sibling, "col": col})
        sector = sector_ref[slot]
        start = offset_ref[row, sector]
        end = jnp.where(sector == 15, ROWS, offset_ref[row, jnp.minimum(sector + 1, 15)])
        count = end - start
        for k in range(0, NMAX // 16, 2):
            both = th[pl.ds(start + 16 * k, 32)].reshape(512, LANES)
            both = jnp.concatenate([both[:256], both[256:]], axis=1)
            gated = jnp.dot(bd[...], both, preferred_element_type=jnp.float32)
            gated = jnp.where(state + 16 * k < count, gated, 0.0).astype(jnp.bfloat16)
            for a in range(SITES):
                for b in range(SITES):
                    for m in range(2):
                        ap[a * NMAX + 16 * (k + m): a * NMAX + 16 * (k + m + 1), b * LANES:(b + 1) * LANES] = gated[
                            (a * 4 + b) * 16:(a * 4 + b + 1) * 16, m * LANES:(m + 1) * LANES]
        product = jnp.dot(ap[...], vall[place, s], preferred_element_type=jnp.float32).astype(jnp.bfloat16)
        for a in range(SITES):
            part[u, a] = product[a * NMAX:(a + 1) * NMAX]
        axis = u % 2
        mine = z if axis == 0 else y
        far = (mine + 2) % 4
        send(part.at[u, far, pl.ds(0, HALF)], half_in.at[u, 0], half_send.at[u, 0], half_recv.at[u, 0], along(axis, 1))
        send(part.at[u, far, pl.ds(HALF, HALF)], half_in.at[u, 1], half_send.at[u, 1], half_recv.at[u, 1], along(axis, 3))

    def pass_on(u):
        axis = u % 2
        mine = z if axis == 0 else y
        for n, step in ((0, 1), (1, 3)):
            arrived(half_in.at[u, n], half_recv.at[u, n])
            to = (mine + step) % 4
            rows = pl.ds(n * HALF, HALF)
            total = part[u, to, rows, :].astype(jnp.float32) + half_in[u, n].astype(jnp.float32)
            part[u, to, rows, :] = total.astype(jnp.bfloat16)
            send(part.at[u, to], ring_in.at[u, n], ring_send.at[u, n], ring_recv.at[u, n], along(axis, step))

    def split(u):
        axis = u % 2
        mine = z if axis == 0 else y
        second = y if axis == 0 else z
        for n in range(2):
            arrived(ring_in.at[u, n], ring_recv.at[u, n])
        total = part[u, mine].astype(jnp.float32) + ring_in[u, 0].astype(jnp.float32) + ring_in[u, 1].astype(jnp.float32)
        total = total.astype(jnp.bfloat16)
        for q in range(4):
            quart[u, q] = total[:, q * LANES:(q + 1) * LANES]
        for d in (2, 1, 3):
            send(quart.at[u, (second + d) % 4], quart_in.at[u, d - 1], quart_send.at[u, d - 1],
                 quart_recv.at[u, d - 1], along(1 - axis, d))

    def finish(u):
        axis = u % 2
        place, s = ORDER[u]
        mine = z if axis == 0 else y
        second = y if axis == 0 else z
        total = quart[u, second].astype(jnp.float32)
        for d in (1, 2, 3):
            arrived(quart_in.at[u, d - 1], quart_recv.at[u, d - 1])
            total = total + quart_in[u, d - 1].astype(jnp.float32)
        done[u] = total.astype(jnp.bfloat16)
        for h in range(2):
            src = done.at[u, pl.ds(h * HALF, HALF)]
            dst = fin_ref.at[s, mine, second]
            target = 2 * row + h
            if place == 0:
                @pl.when(col == target)
                def _():
                    pltpu.make_async_copy(src, dst, fin_recv.at[s, col]).start()

                @pl.when(col != target)
                def _():
                    pltpu.make_async_remote_copy(
                        src_ref=src, dst_ref=dst, send_sem=fin_send.at[u, h], recv_sem=fin_recv.at[s, col],
                        device_id={"row": places[place], "col": target}, device_id_type=MESH).start()
            else:
                send(src, dst, fin_send.at[u, h], fin_recv.at[s, col], {"row": places[place], "col": target})

    for step in range(UNITS + LAG[2]):
        if step < UNITS:
            compute(step)
        if 0 <= step - LAG[0] < UNITS:
            pass_on(step - LAG[0])
        if 0 <= step - LAG[1] < UNITS:
            split(step - LAG[1])
        if 0 <= step - LAG[2] < UNITS:
            finish(step - LAG[2])

    for s in range(2):
        @pl.loop(0, 16)
        def _(c):
            arrived(fin_ref.at[s, 0, 0], fin_recv.at[s, c])

    for copy in sends:
        copy.wait_send()
    for s in range(2):
        for h in range(2):
            @pl.when(col != 2 * row + h)
            def _():
                pltpu.make_async_copy(done.at[s, pl.ds(h * HALF, HALF)], done.at[s, pl.ds(h * HALF, HALF)], fin_send.at[s, h]).wait()


def project(theta, gate, vectors, slot_sector, block_offsets):
    bf = jnp.bfloat16
    dma = pltpu.SemaphoreType.DMA
    vmem = pl.BlockSpec(memory_space=pltpu.VMEM)
    smem = pl.BlockSpec(memory_space=pltpu.SMEM)
    hbm = pl.BlockSpec(memory_space=pl.ANY)
    return pl.pallas_call(
        project_kernel,
        out_shape=jax.ShapeDtypeStruct((2, SITES, 4, HALF, LANES), bf),
        in_specs=[hbm, vmem, hbm, smem, smem],
        out_specs=vmem,
        scratch_shapes=[
            pltpu.VMEM((ROWS + NMAX, 16, LANES), bf),
            pltpu.VMEM((256, 256), bf),
            pltpu.VMEM((SITES * NMAX, KEPT), bf),
            pltpu.VMEM((8, 2, KEPT, KEPT), bf),
            pltpu.VMEM((UNITS, SITES, NMAX, KEPT), bf),
            pltpu.VMEM((UNITS, 2, HALF, KEPT), bf),
            pltpu.VMEM((UNITS, 2, NMAX, KEPT), bf),
            pltpu.VMEM((UNITS, 4, NMAX, LANES), bf),
            pltpu.VMEM((UNITS, 3, NMAX, LANES), bf),
            pltpu.VMEM((UNITS, NMAX, LANES), bf),
            dma, dma, dma((14,)), dma((8, 2)),
            dma((UNITS, 2)), dma((UNITS, 2)), dma((UNITS, 2)), dma((UNITS, 2)),
            dma((UNITS, 3)), dma((UNITS, 3)), dma((UNITS, 2)), dma((2, 16)),
        ],
        compiler_params=pltpu.CompilerParams(has_side_effects=True, vmem_limit_bytes=56 * 2**20),
        cost_estimate=pl.CostEstimate(flops=5_000_000_000, bytes_accessed=6_000_000, transcendentals=0),
        name="project",
    )(theta, gate, vectors, slot_sector, block_offsets)


def refine_step(gram_matrix, correlation, gram_diag, corr_diag, kept_rank):
    kept_most = gram_matrix.shape[0]
    identity = jnp.eye(kept_most, dtype=jnp.float32)
    lambdas = gram_diag / (corr_diag + 1e-06)
    resid = identity - correlation
    differ = lambdas[None, :] - lambdas[:, None]
    divisor = differ * differ + (DAMPING * (lambdas[:, None] + lambdas[None, :])) ** 2 + 1e-06
    offdiag = (gram_matrix + lambdas[None, :] * resid) * differ / divisor
    indices = jnp.arange(kept_most)
    inside = (indices[:, None] < kept_rank) & (indices[None, :] < kept_rank)
    result = jnp.where(identity > 0.5, 0.5 * resid, offdiag)
    return jnp.where(inside, result, jnp.float32(0.0))


def shards(theta, gate, warm_start, slot_sector, kept, block_offsets):
    my_row = lax.axis_index("row")
    vectors = warm_start.reshape(2, KEPT, KEPT)
    fin = project(theta.reshape(ROWS, 16, LANES), gate.reshape(16, 16), vectors, slot_sector, block_offsets)
    projected_b = fin.transpose(0, 1, 3, 2, 4).reshape(2, SITES * HALF, KEPT)
    correlation_part = jnp.einsum("snk,snl->skl", vectors, vectors, preferred_element_type=jnp.float32)
    gram_part = jnp.einsum("snk,snl->skl", projected_b, projected_b, preferred_element_type=jnp.float32)
    correlation = lax.psum(correlation_part, "col")
    gram_matrix = lax.psum(gram_part, "col")
    my_sectors = lax.dynamic_slice_in_dim(slot_sector, my_row * 2, 2, 0)
    my_chooser = (my_sectors[:, None] == jnp.arange(16, dtype=jnp.int32)[None, :]).astype(jnp.int32)
    my_kept = jnp.sum(my_chooser * kept[None, :], axis=1)
    identity = jnp.eye(KEPT, dtype=jnp.float32)[None]
    gram_diag = jnp.sum(gram_matrix * identity, axis=1)
    corr_diag = jnp.sum(correlation * identity, axis=1)
    corr_b = jax.vmap(refine_step)(gram_matrix, correlation, gram_diag, corr_diag, my_kept).astype(jnp.bfloat16)
    kept_mask = (jnp.arange(KEPT)[None, :] < my_kept[:, None]).astype(jnp.float32)
    new_vectors = vectors.astype(jnp.float32) + jnp.einsum(
        "snk,skl->snl", vectors, corr_b, preferred_element_type=jnp.float32
    )
    new_vectors = new_vectors * kept_mask[:, None, :]
    left = projected_b.astype(jnp.float32) + jnp.einsum(
        "snk,skl->snl", projected_b, corr_b, preferred_element_type=jnp.float32
    )
    left = left * kept_mask[:, None, :]
    left = left.reshape(2, SITES, HALF, KEPT).transpose(2, 0, 1, 3)
    return (left, new_vectors.reshape(2, 4, LANES, KEPT))


def solution(mesh):
    in_specs = (P("row", None, None, "col"), P(), P("row", None, "col", None), P(), P(), P())
    out_specs = (P("col", "row", None, None), P("row", None, "col", None))
    return jax.shard_map(shards, mesh=mesh, in_specs=in_specs, out_specs=out_specs, check_vma=False)
```

time: 347 us -> 214 us (0.62)
  waiting for transfers between devices: 196 us -> 106 us
  blocking collectives: 77.7 us -> 0 us
  Pallas kernels: 0 us -> 75.8 us
  local copies, waits for them, and re-layouts: 30.9 us -> 5.2 us
  matrix products: 20.2 us -> 7.85 us
    reduce_scatter x1 -> x0, waiting for transfers between devices: 93.4 us -> none  [shards(): lax.psum_scatter(jnp.einsum('istn,snk->istk', blocks, vectors, preferred_...]
    all_to_all x1 -> x0, blocking collectives: 77.7 us -> none  [shards(): lax.all_to_all(outgoing, 'row', split_axis=1, concat_axis=0, tiled=True)]
    pallas_call x0 -> x1, Pallas kernels: none -> 75.8 us  [project(): pl.pallas_call(project_kernel, out_shape=jax.ShapeDtypeStruct((2, SITES,...]
    gather x2 -> x0, local copies, waits for them, and re-layouts: 14.9 us -> none  [shards(): gated[row_index]]
    dot_general x4 -> x2, matrix products: 16 us -> 2.18 us  [the longest x1 1.81 us: shards(): jnp.einsum('snk,snl->skl', projected_b, projected_b, preferred_element_ty...]
    reshape x1 -> x3, local copies, waits for them, and re-layouts: 7.22 us -> 2.94 us  [the longest x1 1.4 us: shards(): gate.reshape(16, 16)]
    psum x1, waiting for transfers between devices: 102 us -> 106 us  [shards(): gram_matrix = lax.psum(gram_part, 'col')]
    select_n x2 -> x0, local copies, waits for them, and re-layouts: 3.66 us -> none  [the longest x1 3.58 us: shards(): jnp.where(live_mask[:, :, None, None], gated[row_index], jnp.zeros((), jn...]
  transfers between devices with their start and end apart: 2 -> 1, of which waited for: 2 -> 1; matrix products, arithmetic and copies ran while one was open for 1% -> 0% of each run, Pallas kernels for 0% -> 0%
where the time goes in v2:
time: 214 us
  waiting for transfers between devices  106 us (50%)
  Pallas kernels  75.8 us (35%)
  between operations  14.1 us (7%)
  matrix products  7.85 us (4%)
  local copies, waits for them, and re-layouts  5.2 us (2%)
  other arithmetic  5.01 us (2%)
    psum x1, waiting for transfers between devices, shards(): gram_matrix = lax.psum(gram_part, 'col')  106 us
    pallas_call x1, Pallas kernels, project(): pl.pallas_call(project_kernel, out_shape=jax.ShapeDtypeStruct((2, SITES,...  75.8 us
  transfers between devices with their start and end apart: 1, of which 1 were waited for; matrix products, arithmetic and copies ran while one was open for 0% of the time, Pallas kernels for 0%

profile of v2, /device:TPU:1, one launch (start us, length us, event | category | flops | bytes accessed | tf_op | source)
XLA Modules:
  0.0 214.1 jit_solution(10105491349609561187)
XLA Ops:
  7.2 0.0 all-reduce.3.cloned.1.call-start
  7.2 1.4 reshape.106.gate_ref
  8.6 3.6 %fusion.11 = f32[2,512,512]{2,1,0:T(8,128)} fusion(bf16[2,512,512]{2,1,0:T(8,128)(2,1)} %bitcast.20), kind=kOutput, calls=%fused_computation.23 | convolution fusion | flops 536870912 | bytes 3145728 | tf_op jit(solution)/shard_map/snk,snl->skl/dot_general | solution.py:252
  12.2 75.8 %project.1 = bf16[2,4,4,48,128]{4,3,2,1,0:T(8,128)(2,1)} custom-call(bf16[1024,16,128]{2,1,0:T(8,128)(2,1)} %bitcast.27, bf16[16,16]{1,0:T(8,128)(2,1)} %reshape.106.gate_ref, bf16[2,512,512]{2,1,0:T(8,128)(2,1)} %bitcast.21, s32[16]{0:T(128)} %sector_ref.1, s32[8,16]{1,0:T(8,128)} %offset_ref.1), custom_call_target="tpu_custom_call" | custom-call | flops 5000000000 | bytes 6000000 | tf_op jit(solution)/shard_map/project/pallas_call | solution.py:207
  88.1 1.2 copy.13
  89.2 0.2 reshape.108
  89.4 1.8 fusion.12
  91.2 0.0 copy-start.3
  91.2 0.0 all-reduce.3.cloned.1.call-update
  91.2 0.6 copy-done.3
  91.9 0.1 dynamic_slice.3
  91.9 0.0 copy-done.4
  91.9 0.2 fusion.9
  92.1 0.2 fusion.8
  92.3 0.1 fusion.10
  92.4 106.0 %all-reduce.3.cloned.1.call-done = (f32[2,512,512]{2,1,0:T(8,128)}, f32[2,512,512]{2,1,0:T(8,128)}) async-done(((f32[2,512,512]{2,1,0:T(8,128)}, f32[2,512,512]{2,1,0:T(8,128)}), (f32[2,512,512]{2,1,0:T(8,128)}, f32[2,512,512]{2,1,0:T(8,128)})) %all-reduce.3.cloned.1.call-update) | async-done | bytes 4194320 | tf_op jit(solution)/shard_map/psum | solution.py:255
  198.4 3.0 %multiply_reduce_fusion = (f32[2,512]{1,0:T(2,128)S(1)}, f32[2,512]{1,0:T(2,128)S(1)}) fusion(f32[2,512,512]{2,1,0:T(8,128)} %get-tuple-element.5, f32[512,512]{1,0:T(8,128)S(1)} %get-tuple-element.8, f32[2,512,512]{2,1,0:T(8,128)} %get-tuple-element.4), kind=kLoop, calls=%fused_computation.9 | loop fusion | flops 2095104 | bytes 5251072 | tf_op jit(solution)/shard_map/reduce_sum | solution.py:261
  201.5 0.0 copy-done.1
  201.5 0.4 copy-done.2
  201.9 1.5 fusion.6
  203.4 0.0 copy-done
  203.4 2.0 fusion.5
  205.4 0.4 fusion.7
  205.8 1.4 copy.18
  (5 shorter events, 0.0 us)
Async XLA Ops:
  7.2 191.2 %all-reduce.3.cloned.1.call-start = ((), (), s32[]{:S(2)}) async-start(), calls=%async_computation | async-start | bytes 8388608 | tf_op jit(solution)/shard_map/psum | solution.py:255
  91.2 0.7 copy-start.3
  91.2 0.7 copy-start.4
  198.4 3.1 %copy-start.1 = (f32[2,512,512]{2,1,0:T(8,128)S(1)}, f32[2,512,512]{2,1,0:T(8,128)}, u32[]{:S(2)}) copy-start(f32[2,512,512]{2,1,0:T(8,128)} %get-tuple-element.4) | copy-start | bytes 6291460
  198.4 3.5 %copy-start.2 = (f32[2,512,512]{2,1,0:T(8,128)S(1)}, f32[2,512,512]{2,1,0:T(8,128)}, u32[]{:S(2)}) copy-start(f32[2,512,512]{2,1,0:T(8,128)} %get-tuple-element.5) | copy-start | bytes 6291460
  201.9 1.5 copy-start
Sparse Core Ops, SparseCore 0:
  91.4 107.0 all-reduce.2

commit v3 on v2

--- a/solution.py
+++ b/solution.py
@@ -1,5 +1,3 @@
-import functools
-
 import jax
 import jax.numpy as jnp
 from jax import lax
@@ -11,6 +9,7 @@
 HALF = NMAX // 2
 SITES = 4
 LANES = 128
+SHARE = 32
 KEPT = 512
 ROWS = 1024
 DAMPING = 0.25
@@ -26,11 +25,147 @@
 LAG = (2, 4, 6)
 
 
+def overlap(factor, out, diag, row, col):
+    for s in range(2):
+        block = factor[s]
+        product = lax.dot_general(block, block, (((0,), (0,)), ((), ())), preferred_element_type=jnp.float32)
+        product = product.astype(jnp.bfloat16)
+        for c in range(16):
+            out[c, s] = product[c * SHARE:(c + 1) * SHARE]
+        wide = block.astype(jnp.float32)
+        squares = jnp.sum(wide * wide, axis=0, keepdims=True)
+        for q in range(4):
+            diag[col, s * 4 + q:s * 4 + q + 1] = squares[:, q * LANES:(q + 1) * LANES]
+
+
+def start_exchange(out, into, send_sem, recv_sem, row, col):
+    @pl.loop(1, 16)
+    def _(d):
+        to = (col + d) % 16
+        pltpu.make_async_remote_copy(
+            src_ref=out.at[to], dst_ref=into.at[col], send_sem=send_sem.at[to], recv_sem=recv_sem.at[col],
+            device_id={"row": row, "col": to}, device_id_type=MESH).start()
+
+
+def start_shared(both, send_sem, recv_sem, row, col):
+    @pl.loop(1, 16)
+    def _(d):
+        to = (col + d) % 16
+        pltpu.make_async_remote_copy(
+            src_ref=both.at[col], dst_ref=both.at[col], send_sem=send_sem.at[to], recv_sem=recv_sem.at[col],
+            device_id={"row": row, "col": to}, device_id_type=MESH).start()
+
+
+def wait_on(ref, sem):
+    pltpu.make_async_copy(ref, ref, sem).wait()
+
+
+def finish_exchange(out, into, send_sem, recv_sem, col):
+    @pl.loop(1, 16)
+    def _(d):
+        source = (col + d) % 16
+        wait_on(into.at[source], recv_sem.at[source])
+        wait_on(out.at[source], send_sem.at[source])
+
+    into[col] = out[col]
+    total = into[0].astype(jnp.float32)
+    for c in range(1, 16):
+        total = total + into[c].astype(jnp.float32)
+    return total
+
+
+def finish_shared(both, send_sem, recv_sem, col):
+    @pl.loop(1, 16)
+    def _(d):
+        source = (col + d) % 16
+        wait_on(both.at[source], recv_sem.at[source])
+        wait_on(both.at[col], send_sem.at[source])
+
+    return jnp.sum(both[...], axis=0)
+
+
+def refine_kernel(
+    fin_ref, corr_ref, corr_diag_ref, sector_ref, kept_ref, out_ref, mask_ref,
+    factor, gram_out, gram_in, diag_in, gram_send, gram_recv, diag_send, diag_recv, out_send, out_recv,
+):
+    row, col = lax.axis_index("row"), lax.axis_index("col")
+    barrier = pltpu.get_barrier_semaphore()
+
+    @pl.loop(1, 16)
+    def _(d):
+        pl.semaphore_signal(barrier, inc=1, device_id={"row": row, "col": (col + d) % 16}, device_id_type=MESH)
+
+    for s in range(2):
+        for a in range(SITES):
+            for q in range(4):
+                factor[s, a * HALF:(a + 1) * HALF, q * LANES:(q + 1) * LANES] = fin_ref[s, a, q]
+    overlap(factor, gram_out, diag_in, row, col)
+    pl.semaphore_wait(barrier, 15)
+    start_shared(diag_in, diag_send, diag_recv, row, col)
+    start_exchange(gram_out, gram_in, gram_send, gram_recv, row, col)
+    gram_diag = finish_shared(diag_in, diag_send, diag_recv, col)
+    corr_diag = corr_diag_ref[...]
+    lambdas = gram_diag / (corr_diag + 1e-06)
+    gram = finish_exchange(gram_out, gram_in, gram_send, gram_recv, col)
+    at_row = lax.broadcasted_iota(jnp.int32, (SHARE, KEPT), 0) + SHARE * col
+    at_col = lax.broadcasted_iota(jnp.int32, (SHARE, KEPT), 1)
+    for s in range(2):
+        kept = kept_ref[sector_ref[2 * row + s]]
+        across = jnp.concatenate([lambdas[s * 4 + q:s * 4 + q + 1] for q in range(4)], axis=1)
+        norms = jnp.concatenate([corr_diag[s * 4 + q:s * 4 + q + 1] for q in range(4)], axis=1)
+        across = jnp.broadcast_to(across, (SHARE, KEPT))
+        down = jnp.sum(jnp.where(at_row == at_col, across, 0.0), axis=1, keepdims=True)
+        differ = across - down
+        mean = DAMPING * (across + down)
+        divisor = differ * differ + mean * mean + 1e-06
+        offdiag = (gram[s] - across * corr_ref[s]) * differ / divisor
+        result = jnp.where(at_row == at_col, 0.5 * (1.0 - norms), offdiag)
+        result = jnp.where((at_row < kept) & (at_col < kept), result, 0.0)
+        out_ref[s, col] = result.astype(jnp.bfloat16)
+        lanes = lax.broadcasted_iota(jnp.int32, (8, KEPT), 1)
+        mask_ref[s] = jnp.where(lanes < kept, 1.0, 0.0)
+
+    @pl.loop(1, 16)
+    def _(d):
+        to = (col + d) % 16
+        pltpu.make_async_remote_copy(
+            src_ref=out_ref.at[:, col], dst_ref=out_ref.at[:, col], send_sem=out_send.at[to],
+            recv_sem=out_recv.at[col], device_id={"row": row, "col": to}, device_id_type=MESH).start()
+
+    @pl.loop(1, 16)
+    def _(d):
+        source = (col + d) % 16
+        wait_on(out_ref.at[:, source], out_recv.at[source])
+        wait_on(out_ref.at[:, col], out_send.at[source])
+
+
+def refine(fin, correlation, corr_diag, slot_sector, kept):
+    bf = jnp.bfloat16
+    dma = pltpu.SemaphoreType.DMA
+    vmem = pl.BlockSpec(memory_space=pltpu.VMEM)
+    smem = pl.BlockSpec(memory_space=pltpu.SMEM)
+    return pl.pallas_call(
+        refine_kernel,
+        out_shape=(jax.ShapeDtypeStruct((2, 16, SHARE, KEPT), bf), jax.ShapeDtypeStruct((2, 8, KEPT), jnp.float32)),
+        in_specs=[vmem, vmem, vmem, smem, smem],
+        out_specs=(vmem, vmem),
+        scratch_shapes=[
+            pltpu.VMEM((2, SITES * HALF, KEPT), bf),
+            pltpu.VMEM((16, 2, SHARE, KEPT), bf),
+            pltpu.VMEM((16, 2, SHARE, KEPT), bf),
+            pltpu.VMEM((16, 8, LANES), jnp.float32),
+        ] + [dma((16,))] * 6,
+        compiler_params=pltpu.CompilerParams(has_side_effects=True, collective_id=1, vmem_limit_bytes=32 * 2**20),
+        cost_estimate=pl.CostEstimate(flops=200_000_000, bytes_accessed=2_000_000, transcendentals=0),
+        name="refine",
+    )(fin, correlation, corr_diag, slot_sector, kept)
+
+
 def project_kernel(
-    theta_ref, gate_ref, v_ref, sector_ref, offset_ref, fin_ref,
-    th, bd, ap, vall, part, half_in, ring_in, quart, quart_in, done,
+    theta_ref, gate_ref, v_ref, sector_ref, offset_ref, fin_ref, corr_ref, corr_diag_ref,
+    corr_out, corr_in, diag_in, th, bd, ap, vall, part, half_in, ring_in, quart, quart_in, done,
     th_sem, v_sem, v_send, v_recv, half_send, half_recv, ring_send, ring_recv,
-    quart_send, quart_recv, fin_send, fin_recv,
+    quart_send, quart_recv, fin_send, fin_recv, corr_send, corr_recv, diag_send, diag_recv,
 ):
     row, col = lax.axis_index("row"), lax.axis_index("col")
     x, core = row // 2, row % 2
@@ -177,12 +312,19 @@
     for step in range(UNITS + LAG[2]):
         if step < UNITS:
             compute(step)
+        if step == 3:
+            overlap(vall.at[0], corr_out, diag_in, row, col)
+            start_exchange(corr_out, corr_in, corr_send, corr_recv, row, col)
+            start_shared(diag_in, diag_send, diag_recv, row, col)
         if 0 <= step - LAG[0] < UNITS:
             pass_on(step - LAG[0])
         if 0 <= step - LAG[1] < UNITS:
             split(step - LAG[1])
         if 0 <= step - LAG[2] < UNITS:
             finish(step - LAG[2])
+
+    corr_ref[...] = finish_exchange(corr_out, corr_in, corr_send, corr_recv, col)
+    corr_diag_ref[...] = finish_shared(diag_in, diag_send, diag_recv, col)
 
     for s in range(2):
         @pl.loop(0, 16)
@@ -206,10 +348,17 @@
     hbm = pl.BlockSpec(memory_space=pl.ANY)
     return pl.pallas_call(
         project_kernel,
-        out_shape=jax.ShapeDtypeStruct((2, SITES, 4, HALF, LANES), bf),
+        out_shape=(
+            jax.ShapeDtypeStruct((2, SITES, 4, HALF, LANES), bf),
+            jax.ShapeDtypeStruct((2, SHARE, KEPT), jnp.float32),
+            jax.ShapeDtypeStruct((8, LANES), jnp.float32),
+        ),
         in_specs=[hbm, vmem, hbm, smem, smem],
-        out_specs=vmem,
+        out_specs=(vmem, vmem, vmem),
         scratch_shapes=[
+            pltpu.VMEM((16, 2, SHARE, KEPT), bf),
+            pltpu.VMEM((16, 2, SHARE, KEPT), bf),
+            pltpu.VMEM((16, 8, LANES), jnp.float32),
             pltpu.VMEM((ROWS + NMAX, 16, LANES), bf),
             pltpu.VMEM((256, 256), bf),
             pltpu.VMEM((SITES * NMAX, KEPT), bf),
@@ -223,6 +372,7 @@
             dma, dma, dma((14,)), dma((8, 2)),
             dma((UNITS, 2)), dma((UNITS, 2)), dma((UNITS, 2)), dma((UNITS, 2)),
             dma((UNITS, 3)), dma((UNITS, 3)), dma((UNITS, 2)), dma((2, 16)),
+            dma((16,)), dma((16,)), dma((16,)), dma((16,)),
         ],
         compiler_params=pltpu.CompilerParams(has_side_effects=True, vmem_limit_bytes=56 * 2**20),
         cost_estimate=pl.CostEstimate(flops=5_000_000_000, bytes_accessed=6_000_000, transcendentals=0),
@@ -230,37 +380,13 @@
     )(theta, gate, vectors, slot_sector, block_offsets)
 
 
-def refine_step(gram_matrix, correlation, gram_diag, corr_diag, kept_rank):
-    kept_most = gram_matrix.shape[0]
-    identity = jnp.eye(kept_most, dtype=jnp.float32)
-    lambdas = gram_diag / (corr_diag + 1e-06)
-    resid = identity - correlation
-    differ = lambdas[None, :] - lambdas[:, None]
-    divisor = differ * differ + (DAMPING * (lambdas[:, None] + lambdas[None, :])) ** 2 + 1e-06
-    offdiag = (gram_matrix + lambdas[None, :] * resid) * differ / divisor
-    indices = jnp.arange(kept_most)
-    inside = (indices[:, None] < kept_rank) & (indices[None, :] < kept_rank)
-    result = jnp.where(identity > 0.5, 0.5 * resid, offdiag)
-    return jnp.where(inside, result, jnp.float32(0.0))
-
-
 def shards(theta, gate, warm_start, slot_sector, kept, block_offsets):
-    my_row = lax.axis_index("row")
     vectors = warm_start.reshape(2, KEPT, KEPT)
-    fin = project(theta.reshape(ROWS, 16, LANES), gate.reshape(16, 16), vectors, slot_sector, block_offsets)
+    fin, correlation, corr_diag = project(theta.reshape(ROWS, 16, LANES), gate.reshape(16, 16), vectors, slot_sector, block_offsets)
+    corr_b, mask = refine(fin, correlation, corr_diag, slot_sector, kept)
+    corr_b = corr_b.reshape(2, KEPT, KEPT)
+    kept_mask = mask[:, 0]
     projected_b = fin.transpose(0, 1, 3, 2, 4).reshape(2, SITES * HALF, KEPT)
-    correlation_part = jnp.einsum("snk,snl->skl", vectors, vectors, preferred_element_type=jnp.float32)
-    gram_part = jnp.einsum("snk,snl->skl", projected_b, projected_b, preferred_element_type=jnp.float32)
-    correlation = lax.psum(correlation_part, "col")
-    gram_matrix = lax.psum(gram_part, "col")
-    my_sectors = lax.dynamic_slice_in_dim(slot_sector, my_row * 2, 2, 0)
-    my_chooser = (my_sectors[:, None] == jnp.arange(16, dtype=jnp.int32)[None, :]).astype(jnp.int32)
-    my_kept = jnp.sum(my_chooser * kept[None, :], axis=1)
-    identity = jnp.eye(KEPT, dtype=jnp.float32)[None]
-    gram_diag = jnp.sum(gram_matrix * identity, axis=1)
-    corr_diag = jnp.sum(correlation * identity, axis=1)
-    corr_b = jax.vmap(refine_step)(gram_matrix, correlation, gram_diag, corr_diag, my_kept).astype(jnp.bfloat16)
-    kept_mask = (jnp.arange(KEPT)[None, :] < my_kept[:, None]).astype(jnp.float32)
     new_vectors = vectors.astype(jnp.float32) + jnp.einsum(
         "snk,skl->snl", vectors, corr_b, preferred_element_type=jnp.float32
     )

time: 214 us -> 137 us (0.64)
  the two profiles are of different devices: /device:TPU:1 before, /device:TPU:103 now
where the time goes in v3:
time: 137 us; the launch traced here: 136 us
  Pallas kernels  126 us (92%)
  local copies, waits for them, and re-layouts  6.67 us (5%)
  matrix products  2.41 us (2%)
    pallas_call x1, Pallas kernels, project(): pl.pallas_call(project_kernel, out_shape=(jax.ShapeDtypeStruct((2, SITES,...  78.6 us
    pallas_call x1, Pallas kernels, refine(): pl.pallas_call(refine_kernel, out_shape=(jax.ShapeDtypeStruct((2, 16, SHA...  47.9 us

profile of v3, /device:TPU:103, one launch (start us, length us, event | category | flops | bytes accessed | tf_op | source)
XLA Modules:
  0.0 136.3 jit_solution(16527190040581214465)
XLA Ops:
  0.6 1.4 %reshape.26.gate_ref = bf16[16,16]{1,0:T(8,128)(2,1)} reshape(bf16[4,4,4,4]{3,2,1,0:T(4,128)(2,1)} %param.7) | data formatting | bytes 1024 | tf_op jit(solution)/shard_map/reshape | solution.py:385
  2.0 0.0 copy-start.1
  2.0 0.0 copy-start.2
  2.0 78.6 %project.1 = (bf16[2,4,4,48,128]{4,3,2,1,0:T(8,128)(2,1)}, f32[2,32,512]{2,1,0:T(8,128)}, f32[8,128]{1,0:T(8,128)}) custom-call(bf16[1024,16,128]{2,1,0:T(8,128)(2,1)} %bitcast.30, bf16[16,16]{1,0:T(8,128)(2,1)} %reshape.26.gate_ref, bf16[2,512,512]{2,1,0:T(8,128)(2,1)} %bitcast.25, s32[16]{0:T(128)} %sector_ref.3, s32[8,16]{1,0:T(8,128)} %offset_ref.1), custom_call_target="tpu_custom_call" | custom-call | flops 5000000000 | bytes 6000000 | tf_op jit(solution)/shard_map/project/pallas_call | solution.py:349
  80.6 1.2 copy.9
  81.8 0.2 reshape.28
  81.9 0.0 copy-done.1
  81.9 0.0 copy-done.2
  81.9 0.0 copy-start
  81.9 1.0 copy-done
  82.9 0.0 copy-start.3
  82.9 0.9 copy-done.3
  83.8 0.0 copy-start.4
  83.8 0.7 copy-done.4
  84.5 47.9 %refine.1 = (bf16[2,16,32,512]{3,2,1,0:T(8,128)(2,1)S(1)}, f32[2,8,512]{2,1,0:T(8,128)S(1)}) custom-call(bf16[2,4,4,48,128]{4,3,2,1,0:T(8,128)(2,1)S(1)} %copy-done, f32[2,32,512]{2,1,0:T(8,128)S(1)} %copy-done.3, f32[8,128]{1,0:T(8,128)S(1)} %copy-done.4, s32[16]{0:T(128)S(1)} %copy-done.1, s32[16]{0:T(128)S(1)} %copy-done.2), custom_call_target="tpu_custom_call" | custom-call | flops 200000000 | bytes 2000000 | tf_op jit(solution)/shard_map/refine/pallas_call | solution.py:147
  132.4 0.0 copy-start.5
  132.5 0.4 fusion.1
  132.8 1.4 %copy.14 = f32[2,4,48,512]{3,1,0,2:T(4,128)} copy(f32[2,4,48,512]{3,2,1,0:T(8,128)S(1)} %bitcast.23) | data formatting | bytes 1572864 | tf_op jit(solution)/shard_map/reshape | solution.py:398
  134.2 0.0 copy-done.5
  134.2 2.0 %fusion = f32[2,512,512]{2,1,0:T(8,128)} fusion(bf16[2,512,512]{2,1,0:T(8,128)(2,1)S(1)} %bitcast.26, bf16[2,512,512]{2,1,0:T(8,128)(2,1)S(1)} %bitcast.21, f32[2,512]{1,0:T(2,128)S(1)} %bitcast.29), kind=kOutput, calls=%fused_computation.1 | convolution fusion | flops 538443776 | bytes 4198400 | tf_op jit(solution)/shard_map/snk,skl->snl/dot_general | solution.py:390
  (2 shorter events, 0.0 us)
Async XLA Ops:
  2.0 79.9 %copy-start.1 = (s32[16]{0:T(128)S(1)}, s32[16]{0:T(128)}, u32[]{:S(2)}) copy-start(s32[16]{0:T(128)} %sector_ref.3) | copy-start | bytes 196
  2.0 79.9 %copy-start.2 = (s32[16]{0:T(128)S(1)}, s32[16]{0:T(128)}, u32[]{:S(2)}) copy-start(s32[16]{0:T(128)} %kept_ref.1) | copy-start | bytes 196
  81.9 1.0 copy-start
  82.9 0.9 copy-start.3
  83.8 0.7 copy-start.4
  132.4 1.8 %copy-start.5 = (bf16[2,4,128,512]{3,2,1,0:T(8,128)(2,1)S(1)}, bf16[2,4,128,512]{3,2,1,0:T(8,128)(2,1)}, u32[]{:S(2)}) copy-start(bf16[2,4,128,512]{3,2,1,0:T(8,128)(2,1)} %param.8) | copy-start | bytes 3145732

commit v4 on v3

--- a/solution.py
+++ b/solution.py
@@ -22,7 +22,6 @@
     (6, 0), (6, 1), (7, 0), (7, 1),
 )
 UNITS = len(ORDER)
-LAG = (2, 4, 6)
 
 
 def overlap(factor, out, diag, row, col):
@@ -84,88 +83,12 @@
     return jnp.sum(both[...], axis=0)
 
 
-def refine_kernel(
-    fin_ref, corr_ref, corr_diag_ref, sector_ref, kept_ref, out_ref, mask_ref,
-    factor, gram_out, gram_in, diag_in, gram_send, gram_recv, diag_send, diag_recv, out_send, out_recv,
-):
-    row, col = lax.axis_index("row"), lax.axis_index("col")
-    barrier = pltpu.get_barrier_semaphore()
-
-    @pl.loop(1, 16)
-    def _(d):
-        pl.semaphore_signal(barrier, inc=1, device_id={"row": row, "col": (col + d) % 16}, device_id_type=MESH)
-
-    for s in range(2):
-        for a in range(SITES):
-            for q in range(4):
-                factor[s, a * HALF:(a + 1) * HALF, q * LANES:(q + 1) * LANES] = fin_ref[s, a, q]
-    overlap(factor, gram_out, diag_in, row, col)
-    pl.semaphore_wait(barrier, 15)
-    start_shared(diag_in, diag_send, diag_recv, row, col)
-    start_exchange(gram_out, gram_in, gram_send, gram_recv, row, col)
-    gram_diag = finish_shared(diag_in, diag_send, diag_recv, col)
-    corr_diag = corr_diag_ref[...]
-    lambdas = gram_diag / (corr_diag + 1e-06)
-    gram = finish_exchange(gram_out, gram_in, gram_send, gram_recv, col)
-    at_row = lax.broadcasted_iota(jnp.int32, (SHARE, KEPT), 0) + SHARE * col
-    at_col = lax.broadcasted_iota(jnp.int32, (SHARE, KEPT), 1)
-    for s in range(2):
-        kept = kept_ref[sector_ref[2 * row + s]]
-        across = jnp.concatenate([lambdas[s * 4 + q:s * 4 + q + 1] for q in range(4)], axis=1)
-        norms = jnp.concatenate([corr_diag[s * 4 + q:s * 4 + q + 1] for q in range(4)], axis=1)
-        across = jnp.broadcast_to(across, (SHARE, KEPT))
-        down = jnp.sum(jnp.where(at_row == at_col, across, 0.0), axis=1, keepdims=True)
-        differ = across - down
-        mean = DAMPING * (across + down)
-        divisor = differ * differ + mean * mean + 1e-06
-        offdiag = (gram[s] - across * corr_ref[s]) * differ / divisor
-        result = jnp.where(at_row == at_col, 0.5 * (1.0 - norms), offdiag)
-        result = jnp.where((at_row < kept) & (at_col < kept), result, 0.0)
-        out_ref[s, col] = result.astype(jnp.bfloat16)
-        lanes = lax.broadcasted_iota(jnp.int32, (8, KEPT), 1)
-        mask_ref[s] = jnp.where(lanes < kept, 1.0, 0.0)
-
-    @pl.loop(1, 16)
-    def _(d):
-        to = (col + d) % 16
-        pltpu.make_async_remote_copy(
-            src_ref=out_ref.at[:, col], dst_ref=out_ref.at[:, col], send_sem=out_send.at[to],
-            recv_sem=out_recv.at[col], device_id={"row": row, "col": to}, device_id_type=MESH).start()
-
-    @pl.loop(1, 16)
-    def _(d):
-        source = (col + d) % 16
-        wait_on(out_ref.at[:, source], out_recv.at[source])
-        wait_on(out_ref.at[:, col], out_send.at[source])
-
-
-def refine(fin, correlation, corr_diag, slot_sector, kept):
-    bf = jnp.bfloat16
-    dma = pltpu.SemaphoreType.DMA
-    vmem = pl.BlockSpec(memory_space=pltpu.VMEM)
-    smem = pl.BlockSpec(memory_space=pltpu.SMEM)
-    return pl.pallas_call(
-        refine_kernel,
-        out_shape=(jax.ShapeDtypeStruct((2, 16, SHARE, KEPT), bf), jax.ShapeDtypeStruct((2, 8, KEPT), jnp.float32)),
-        in_specs=[vmem, vmem, vmem, smem, smem],
-        out_specs=(vmem, vmem),
-        scratch_shapes=[
-            pltpu.VMEM((2, SITES * HALF, KEPT), bf),
-            pltpu.VMEM((16, 2, SHARE, KEPT), bf),
-            pltpu.VMEM((16, 2, SHARE, KEPT), bf),
-            pltpu.VMEM((16, 8, LANES), jnp.float32),
-        ] + [dma((16,))] * 6,
-        compiler_params=pltpu.CompilerParams(has_side_effects=True, collective_id=1, vmem_limit_bytes=32 * 2**20),
-        cost_estimate=pl.CostEstimate(flops=200_000_000, bytes_accessed=2_000_000, transcendentals=0),
-        name="refine",
-    )(fin, correlation, corr_diag, slot_sector, kept)
-
-
 def project_kernel(
-    theta_ref, gate_ref, v_ref, sector_ref, offset_ref, fin_ref, corr_ref, corr_diag_ref,
-    corr_out, corr_in, diag_in, th, bd, ap, vall, part, half_in, ring_in, quart, quart_in, done,
+    theta_ref, gate_ref, v_ref, sector_ref, offset_ref, kept_ref, fin_ref, out_ref, mask_ref,
+    corr_out, corr_in, corr_diag_in, factor, gram_out, gram_in, gram_diag_in, th, bd, ap, vall, part, half_in, ring_in, quart, quart_in, done,
     th_sem, v_sem, v_send, v_recv, half_send, half_recv, ring_send, ring_recv,
-    quart_send, quart_recv, fin_send, fin_recv, corr_send, corr_recv, diag_send, diag_recv,
+    quart_send, quart_recv, fin_send, fin_recv, corr_send, corr_recv, corr_diag_send, corr_diag_recv,
+    gram_send, gram_recv, gram_diag_send, gram_diag_recv, out_send, out_recv,
 ):
     row, col = lax.axis_index("row"), lax.axis_index("col")
     x, core = row // 2, row % 2
@@ -199,13 +122,32 @@
     def arrived(dst, sem):
         pltpu.make_async_copy(dst, dst, sem).wait()
 
+    barrier = pltpu.get_barrier_semaphore()
+
+    def greet(where):
+        pl.semaphore_signal(barrier, inc=1, device_id=where, device_id_type=MESH)
+
+    for where in (sibling, before, after):
+        greet({"row": where, "col": col})
+
+    @pl.loop(1, 16)
+    def _(d):
+        greet({"row": row, "col": (col + d) % 16})
+
+    @pl.loop(1, 16)
+    def _(d):
+        greet({"row": col // 2, "col": (col + d) % 16})
+
+    home = col // 2 == row
+
+    @pl.when(jnp.logical_not(home))
+    def _():
+        greet({"row": col // 2, "col": col})
+
     theta_in = pltpu.make_async_copy(theta_ref, th.at[pl.ds(0, ROWS)], th_sem)
     theta_in.start()
     v_in = pltpu.make_async_copy(v_ref, vall.at[0], v_sem)
     v_in.start()
-    for s in range(2):
-        for n, (where, place) in enumerate(((sibling, 1), (after, 2), (before, 3))):
-            send(v_ref.at[s], vall.at[place, s], v_send.at[3 * s + n], v_recv.at[place, s], {"row": where, "col": col})
 
     big_r = lax.broadcasted_iota(jnp.int32, (256, 256), 0)
     big_c = lax.broadcasted_iota(jnp.int32, (256, 256), 1)
@@ -215,6 +157,11 @@
     spread = jnp.dot(spread.astype(jnp.bfloat16), right_hot.astype(jnp.bfloat16), preferred_element_type=jnp.float32)
     bd[...] = jnp.where(big_r % 16 == big_c // 16, spread, 0.0).astype(jnp.bfloat16)
     th[pl.ds(ROWS, NMAX)] = jnp.zeros((NMAX, 16, LANES), jnp.bfloat16)
+    pl.semaphore_wait(barrier, jnp.where(home, 33, 34))
+
+    for s in range(2):
+        for n, (where, place) in enumerate(((after, 2), (before, 3), (sibling, 1))):
+            send(v_ref.at[s], vall.at[place, s], v_send.at[3 * s + n], v_recv.at[place, s], {"row": where, "col": col})
     theta_in.wait()
     v_in.wait()
 
@@ -309,27 +256,68 @@
             else:
                 send(src, dst, fin_send.at[u, h], fin_recv.at[s, col], {"row": places[place], "col": target})
 
-    for step in range(UNITS + LAG[2]):
-        if step < UNITS:
-            compute(step)
-        if step == 3:
-            overlap(vall.at[0], corr_out, diag_in, row, col)
+    def each(task, group):
+        if 0 <= group < 4:
+            for u in range(4 * group, 4 * group + 4):
+                task(u)
+
+    for group in range(7):
+        each(compute, group)
+        if group == 0:
+            overlap(vall.at[0], corr_out, corr_diag_in, row, col)
             start_exchange(corr_out, corr_in, corr_send, corr_recv, row, col)
-            start_shared(diag_in, diag_send, diag_recv, row, col)
-        if 0 <= step - LAG[0] < UNITS:
-            pass_on(step - LAG[0])
-        if 0 <= step - LAG[1] < UNITS:
-            split(step - LAG[1])
-        if 0 <= step - LAG[2] < UNITS:
-            finish(step - LAG[2])
-
-    corr_ref[...] = finish_exchange(corr_out, corr_in, corr_send, corr_recv, col)
-    corr_diag_ref[...] = finish_shared(diag_in, diag_send, diag_recv, col)
+            start_shared(corr_diag_in, corr_diag_send, corr_diag_recv, row, col)
+        each(finish, group - 2)
+        each(split, group - 1)
+        each(pass_on, group)
+    correlation = finish_exchange(corr_out, corr_in, corr_send, corr_recv, col)
+    corr_diag = finish_shared(corr_diag_in, corr_diag_send, corr_diag_recv, col)
 
     for s in range(2):
         @pl.loop(0, 16)
         def _(c):
             arrived(fin_ref.at[s, 0, 0], fin_recv.at[s, c])
+
+    for s in range(2):
+        for a in range(SITES):
+            for q in range(4):
+                factor[s, a * HALF:(a + 1) * HALF, q * LANES:(q + 1) * LANES] = fin_ref[s, a, q]
+    overlap(factor, gram_out, gram_diag_in, row, col)
+    start_shared(gram_diag_in, gram_diag_send, gram_diag_recv, row, col)
+    start_exchange(gram_out, gram_in, gram_send, gram_recv, row, col)
+    gram_diag = finish_shared(gram_diag_in, gram_diag_send, gram_diag_recv, col)
+    lambdas = gram_diag / (corr_diag + 1e-06)
+    gram = finish_exchange(gram_out, gram_in, gram_send, gram_recv, col)
+    at_row = lax.broadcasted_iota(jnp.int32, (SHARE, KEPT), 0) + SHARE * col
+    at_col = lax.broadcasted_iota(jnp.int32, (SHARE, KEPT), 1)
+    for s in range(2):
+        kept = kept_ref[sector_ref[2 * row + s]]
+        across = jnp.concatenate([lambdas[s * 4 + q:s * 4 + q + 1] for q in range(4)], axis=1)
+        norms = jnp.concatenate([corr_diag[s * 4 + q:s * 4 + q + 1] for q in range(4)], axis=1)
+        across = jnp.broadcast_to(across, (SHARE, KEPT))
+        down = jnp.sum(jnp.where(at_row == at_col, across, 0.0), axis=1, keepdims=True)
+        differ = across - down
+        mean = DAMPING * (across + down)
+        divisor = differ * differ + mean * mean + 1e-06
+        offdiag = (gram[s] - across * correlation[s]) * differ / divisor
+        result = jnp.where(at_row == at_col, 0.5 * (1.0 - norms), offdiag)
+        result = jnp.where((at_row < kept) & (at_col < kept), result, 0.0)
+        out_ref[s, col] = result.astype(jnp.bfloat16)
+        lanes = lax.broadcasted_iota(jnp.int32, (8, KEPT), 1)
+        mask_ref[s] = jnp.where(lanes < kept, 1.0, 0.0)
+
+    @pl.loop(1, 16)
+    def _(d):
+        to = (col + d) % 16
+        pltpu.make_async_remote_copy(
+            src_ref=out_ref.at[:, col], dst_ref=out_ref.at[:, col], send_sem=out_send.at[to],
+            recv_sem=out_recv.at[col], device_id={"row": row, "col": to}, device_id_type=MESH).start()
+
+    @pl.loop(1, 16)
+    def _(d):
+        source = (col + d) % 16
+        wait_on(out_ref.at[:, source], out_recv.at[source])
+        wait_on(out_ref.at[:, col], out_send.at[source])
 
     for copy in sends:
         copy.wait_send()
@@ -340,7 +328,7 @@
                 pltpu.make_async_copy(done.at[s, pl.ds(h * HALF, HALF)], done.at[s, pl.ds(h * HALF, HALF)], fin_send.at[s, h]).wait()
 
 
-def project(theta, gate, vectors, slot_sector, block_offsets):
+def project(theta, gate, vectors, slot_sector, block_offsets, kept):
     bf = jnp.bfloat16
     dma = pltpu.SemaphoreType.DMA
     vmem = pl.BlockSpec(memory_space=pltpu.VMEM)
@@ -350,12 +338,16 @@
         project_kernel,
         out_shape=(
             jax.ShapeDtypeStruct((2, SITES, 4, HALF, LANES), bf),
-            jax.ShapeDtypeStruct((2, SHARE, KEPT), jnp.float32),
-            jax.ShapeDtypeStruct((8, LANES), jnp.float32),
+            jax.ShapeDtypeStruct((2, 16, SHARE, KEPT), bf),
+            jax.ShapeDtypeStruct((2, 8, KEPT), jnp.float32),
         ),
-        in_specs=[hbm, vmem, hbm, smem, smem],
+        in_specs=[hbm, vmem, hbm, smem, smem, smem],
         out_specs=(vmem, vmem, vmem),
         scratch_shapes=[
+            pltpu.VMEM((16, 2, SHARE, KEPT), bf),
+            pltpu.VMEM((16, 2, SHARE, KEPT), bf),
+            pltpu.VMEM((16, 8, LANES), jnp.float32),
+            pltpu.VMEM((2, SITES * HALF, KEPT), bf),
             pltpu.VMEM((16, 2, SHARE, KEPT), bf),
             pltpu.VMEM((16, 2, SHARE, KEPT), bf),
             pltpu.VMEM((16, 8, LANES), jnp.float32),
@@ -372,18 +364,18 @@
             dma, dma, dma((14,)), dma((8, 2)),
             dma((UNITS, 2)), dma((UNITS, 2)), dma((UNITS, 2)), dma((UNITS, 2)),
             dma((UNITS, 3)), dma((UNITS, 3)), dma((UNITS, 2)), dma((2, 16)),
-            dma((16,)), dma((16,)), dma((16,)), dma((16,)),
-        ],
-        compiler_params=pltpu.CompilerParams(has_side_effects=True, vmem_limit_bytes=56 * 2**20),
+        ] + [dma((16,))] * 10,
+        compiler_params=pltpu.CompilerParams(has_side_effects=True, collective_id=0, vmem_limit_bytes=56 * 2**20),
         cost_estimate=pl.CostEstimate(flops=5_000_000_000, bytes_accessed=6_000_000, transcendentals=0),
         name="project",
-    )(theta, gate, vectors, slot_sector, block_offsets)
+    )(theta, gate, vectors, slot_sector, block_offsets, kept)
 
 
 def shards(theta, gate, warm_start, slot_sector, kept, block_offsets):
     vectors = warm_start.reshape(2, KEPT, KEPT)
-    fin, correlation, corr_diag = project(theta.reshape(ROWS, 16, LANES), gate.reshape(16, 16), vectors, slot_sector, block_offsets)
-    corr_b, mask = refine(fin, correlation, corr_diag, slot_sector, kept)
+    fin, corr_b, mask = project(
+        theta.reshape(ROWS, 16, LANES), gate.reshape(16, 16), vectors, slot_sector, block_offsets, kept
+    )
     corr_b = corr_b.reshape(2, KEPT, KEPT)
     kept_mask = mask[:, 0]
     projected_b = fin.transpose(0, 1, 3, 2, 4).reshape(2, SITES * HALF, KEPT)

time: 137 us -> 127 us (0.927)
  the two profiles are of different devices: /device:TPU:103 before, /device:TPU:86 now
where the time goes in v4:
time: 127 us
  Pallas kernels  117 us (92%)
  local copies, waits for them, and re-layouts  5.01 us (4%)
  matrix products  3.63 us (3%)
    pallas_call x1, Pallas kernels, project(): pl.pallas_call(project_kernel, out_shape=(jax.ShapeDtypeStruct((2, SITES,...  117 us

profile of v4, /device:TPU:86, one launch (start us, length us, event | category | flops | bytes accessed | tf_op | source)
XLA Modules:
  0.0 126.6 jit_solution(10884057565521722558)
XLA Ops:
  0.6 1.4 %reshape.26.gate_ref = bf16[16,16]{1,0:T(8,128)(2,1)} reshape(bf16[4,4,4,4]{3,2,1,0:T(4,128)(2,1)} %param.7) | data formatting | bytes 1024 | tf_op jit(solution)/shard_map/reshape | solution.py:377
  2.0 117.3 %project.1 = (bf16[2,4,4,48,128]{4,3,2,1,0:T(8,128)(2,1)}, bf16[2,16,32,512]{3,2,1,0:T(8,128)(2,1)}, f32[2,8,512]{2,1,0:T(8,128)}) custom-call(bf16[1024,16,128]{2,1,0:T(8,128)(2,1)} %bitcast.30, bf16[16,16]{1,0:T(8,128)(2,1)} %reshape.26.gate_ref, bf16[2,512,512]{2,1,0:T(8,128)(2,1)} %bitcast.24, s32[16]{0:T(128)} %sector_ref.1, s32[8,16]{1,0:T(8,128)} %offset_ref.1, ...), custom_call_target="tpu_custom_call" | custom-call | flops 5000000000 | bytes 6000000 | tf_op jit(solution)/shard_map/project/pallas_call | solution.py:337
  119.4 1.2 copy.9
  120.5 0.2 reshape.28
  120.7 0.0 copy-start
  120.7 0.0 copy-start.1
  120.7 0.9 slice.3
  121.6 1.6 %fusion.1 = f32[2,192,512]{2,1,0:T(8,128)S(1)} fusion(bf16[2,192,512]{2,1,0:T(8,128)(2,1)S(1)} %reshape.28, bf16[2,512,512]{2,1,0:T(8,128)(2,1)} %bitcast.20, f32[2,512]{1,0:T(2,128)S(1)} %bitcast.28), kind=kOutput, calls=%fused_computation.3 | convolution fusion | flops 201916416 | bytes 2232320 | tf_op jit(solution)/shard_map/snk,skl->snl/dot_general | solution.py:386
  123.2 1.4 %copy.14 = f32[2,4,48,512]{3,1,0,2:T(4,128)} copy(f32[2,4,48,512]{3,2,1,0:T(8,128)S(1)} %bitcast.22) | data formatting | bytes 1572864 | tf_op jit(solution)/shard_map/reshape | solution.py:390
  124.6 0.0 copy-done
  124.6 0.0 copy-done.1
  124.6 2.0 %fusion = f32[2,512,512]{2,1,0:T(8,128)} fusion(bf16[2,512,512]{2,1,0:T(8,128)(2,1)S(1)} %bitcast.25, bf16[2,512,512]{2,1,0:T(8,128)(2,1)S(1)} %bitcast.21, f32[2,512]{1,0:T(2,128)S(1)} %bitcast.29), kind=kOutput, calls=%fused_computation.1 | convolution fusion | flops 538443776 | bytes 4198400 | tf_op jit(solution)/shard_map/snk,skl->snl/dot_general | solution.py:382
  (1 shorter events, 0.0 us)
Async XLA Ops:
  120.7 3.9 %copy-start = (bf16[2,16,32,512]{3,2,1,0:T(8,128)(2,1)S(1)}, bf16[2,16,32,512]{3,2,1,0:T(8,128)(2,1)}, u32[]{:S(2)}) copy-start(bf16[2,16,32,512]{3,2,1,0:T(8,128)(2,1)} %get-tuple-element.6) | copy-start | bytes 3145732
  120.7 3.9 %copy-start.1 = (bf16[2,4,128,512]{3,2,1,0:T(8,128)(2,1)S(1)}, bf16[2,4,128,512]{3,2,1,0:T(8,128)(2,1)}, u32[]{:S(2)}) copy-start(bf16[2,4,128,512]{3,2,1,0:T(8,128)(2,1)} %param.8) | copy-start | bytes 3145732

commit v5 on v4

--- a/solution.py
+++ b/solution.py
@@ -16,25 +16,23 @@
 MESH = pl.DeviceIdType.MESH
 
 ORDER = (
-    (0, 0), (0, 1), (1, 0), (1, 1),
+    (0, 0), (1, 0), (0, 1), (1, 1),
     (2, 0), (3, 0), (4, 0), (5, 0),
-    (2, 1), (3, 1), (4, 1), (5, 1),
-    (6, 0), (6, 1), (7, 0), (7, 1),
+    (6, 0), (7, 0), (3, 1), (5, 1),
+    (2, 1), (6, 1), (4, 1), (7, 1),
 )
 UNITS = len(ORDER)
 
 
-def overlap(factor, out, diag, row, col):
-    for s in range(2):
-        block = factor[s]
-        product = lax.dot_general(block, block, (((0,), (0,)), ((), ())), preferred_element_type=jnp.float32)
-        product = product.astype(jnp.bfloat16)
-        for c in range(16):
-            out[c, s] = product[c * SHARE:(c + 1) * SHARE]
-        wide = block.astype(jnp.float32)
-        squares = jnp.sum(wide * wide, axis=0, keepdims=True)
-        for q in range(4):
-            diag[col, s * 4 + q:s * 4 + q + 1] = squares[:, q * LANES:(q + 1) * LANES]
+def overlap(block, out, diag, col):
+    product = lax.dot_general(block, block, (((0,), (0,)), ((), ())), preferred_element_type=jnp.float32)
+    product = product.astype(jnp.bfloat16)
+    for c in range(16):
+        out[c] = product[c * SHARE:(c + 1) * SHARE]
+    wide = block.astype(jnp.float32)
+    squares = jnp.sum(wide * wide, axis=0, keepdims=True)
+    for q in range(4):
+        diag[col, q:q + 1] = squares[:, q * LANES:(q + 1) * LANES]
 
 
 def start_exchange(out, into, send_sem, recv_sem, row, col):
@@ -159,9 +157,12 @@
     th[pl.ds(ROWS, NMAX)] = jnp.zeros((NMAX, 16, LANES), jnp.bfloat16)
     pl.semaphore_wait(barrier, jnp.where(home, 33, 34))
 
-    for s in range(2):
-        for n, (where, place) in enumerate(((after, 2), (before, 3), (sibling, 1))):
-            send(v_ref.at[s], vall.at[place, s], v_send.at[3 * s + n], v_recv.at[place, s], {"row": where, "col": col})
+    def send_own(s, n):
+        where, place = ((after, 2), (before, 3), (sibling, 1))[n]
+        send(v_ref.at[s], vall.at[place, s], v_send.at[3 * s + n], v_recv.at[place, s], {"row": where, "col": col})
+
+    for s, n in ((0, 2), (0, 0), (0, 1), (1, 2)):
+        send_own(s, n)
     theta_in.wait()
     v_in.wait()
 
@@ -261,63 +262,78 @@
             for u in range(4 * group, 4 * group + 4):
                 task(u)
 
-    for group in range(7):
-        each(compute, group)
-        if group == 0:
-            overlap(vall.at[0], corr_out, corr_diag_in, row, col)
-            start_exchange(corr_out, corr_in, corr_send, corr_recv, row, col)
-            start_shared(corr_diag_in, corr_diag_send, corr_diag_recv, row, col)
-        each(finish, group - 2)
-        each(split, group - 1)
-        each(pass_on, group)
-    correlation = finish_exchange(corr_out, corr_in, corr_send, corr_recv, col)
-    corr_diag = finish_shared(corr_diag_in, corr_diag_send, corr_diag_recv, col)
-
-    for s in range(2):
+    at_row = lax.broadcasted_iota(jnp.int32, (SHARE, KEPT), 0) + SHARE * col
+    at_col = lax.broadcasted_iota(jnp.int32, (SHARE, KEPT), 1)
+
+    def start_corr():
+        for s in range(2):
+            overlap(vall[0, s], corr_out.at[s], corr_diag_in.at[s], col)
+            start_shared(corr_diag_in.at[s], corr_diag_send.at[s], corr_diag_recv.at[s], row, col)
+            start_exchange(corr_out.at[s], corr_in.at[s], corr_send.at[s], corr_recv.at[s], row, col)
+
+    def start_gram(s):
         @pl.loop(0, 16)
         def _(c):
             arrived(fin_ref.at[s, 0, 0], fin_recv.at[s, c])
 
-    for s in range(2):
         for a in range(SITES):
             for q in range(4):
                 factor[s, a * HALF:(a + 1) * HALF, q * LANES:(q + 1) * LANES] = fin_ref[s, a, q]
-    overlap(factor, gram_out, gram_diag_in, row, col)
-    start_shared(gram_diag_in, gram_diag_send, gram_diag_recv, row, col)
-    start_exchange(gram_out, gram_in, gram_send, gram_recv, row, col)
-    gram_diag = finish_shared(gram_diag_in, gram_diag_send, gram_diag_recv, col)
-    lambdas = gram_diag / (corr_diag + 1e-06)
-    gram = finish_exchange(gram_out, gram_in, gram_send, gram_recv, col)
-    at_row = lax.broadcasted_iota(jnp.int32, (SHARE, KEPT), 0) + SHARE * col
-    at_col = lax.broadcasted_iota(jnp.int32, (SHARE, KEPT), 1)
-    for s in range(2):
+        overlap(factor[s], gram_out.at[s], gram_diag_in.at[s], col)
+        start_shared(gram_diag_in.at[s], gram_diag_send.at[s], gram_diag_recv.at[s], row, col)
+        start_exchange(gram_out.at[s], gram_in.at[s], gram_send.at[s], gram_recv.at[s], row, col)
+
+    def refine(s):
+        correlation = finish_exchange(corr_out.at[s], corr_in.at[s], corr_send.at[s], corr_recv.at[s], col)
+        corr_diag = finish_shared(corr_diag_in.at[s], corr_diag_send.at[s], corr_diag_recv.at[s], col)
+        gram_diag = finish_shared(gram_diag_in.at[s], gram_diag_send.at[s], gram_diag_recv.at[s], col)
+        lambdas = gram_diag / (corr_diag + 1e-06)
+        gram = finish_exchange(gram_out.at[s], gram_in.at[s], gram_send.at[s], gram_recv.at[s], col)
         kept = kept_ref[sector_ref[2 * row + s]]
-        across = jnp.concatenate([lambdas[s * 4 + q:s * 4 + q + 1] for q in range(4)], axis=1)
-        norms = jnp.concatenate([corr_diag[s * 4 + q:s * 4 + q + 1] for q in range(4)], axis=1)
+        across = jnp.concatenate([lambdas[q:q + 1] for q in range(4)], axis=1)
+        norms = jnp.concatenate([corr_diag[q:q + 1] for q in range(4)], axis=1)
         across = jnp.broadcast_to(across, (SHARE, KEPT))
         down = jnp.sum(jnp.where(at_row == at_col, across, 0.0), axis=1, keepdims=True)
         differ = across - down
         mean = DAMPING * (across + down)
         divisor = differ * differ + mean * mean + 1e-06
-        offdiag = (gram[s] - across * correlation[s]) * differ / divisor
+        offdiag = (gram - across * correlation) * differ / divisor
         result = jnp.where(at_row == at_col, 0.5 * (1.0 - norms), offdiag)
         result = jnp.where((at_row < kept) & (at_col < kept), result, 0.0)
         out_ref[s, col] = result.astype(jnp.bfloat16)
         lanes = lax.broadcasted_iota(jnp.int32, (8, KEPT), 1)
         mask_ref[s] = jnp.where(lanes < kept, 1.0, 0.0)
-
-    @pl.loop(1, 16)
-    def _(d):
-        to = (col + d) % 16
-        pltpu.make_async_remote_copy(
-            src_ref=out_ref.at[:, col], dst_ref=out_ref.at[:, col], send_sem=out_send.at[to],
-            recv_sem=out_recv.at[col], device_id={"row": row, "col": to}, device_id_type=MESH).start()
-
-    @pl.loop(1, 16)
-    def _(d):
-        source = (col + d) % 16
-        wait_on(out_ref.at[:, source], out_recv.at[source])
-        wait_on(out_ref.at[:, col], out_send.at[source])
+        start_shared(out_ref.at[s], out_send.at[s], out_recv.at[s], row, col)
+
+    each(compute, 0)
+    start_corr()
+    each(pass_on, 0)
+    send_own(1, 1)
+    each(compute, 1)
+    each(split, 0)
+    send_own(1, 0)
+    each(pass_on, 1)
+    each(finish, 0)
+    each(compute, 2)
+    each(split, 1)
+    each(pass_on, 2)
+    each(finish, 1)
+    each(split, 2)
+    each(compute, 3)
+    each(finish, 2)
+    each(pass_on, 3)
+    start_gram(0)
+    each(split, 3)
+    each(finish, 3)
+    refine(0)
+    start_gram(1)
+    refine(1)
+    for s in range(2):
+        @pl.loop(1, 16)
+        def _(d):
+            source = (col + d) % 16
+            wait_on(out_ref.at[s, source], out_recv.at[s, source])
+            wait_on(out_ref.at[s, col], out_send.at[s, source])
 
     for copy in sends:
         copy.wait_send()
@@ -325,7 +341,7 @@
         for h in range(2):
             @pl.when(col != 2 * row + h)
             def _():
-                pltpu.make_async_copy(done.at[s, pl.ds(h * HALF, HALF)], done.at[s, pl.ds(h * HALF, HALF)], fin_send.at[s, h]).wait()
+                pltpu.make_async_copy(done.at[s, pl.ds(h * HALF, HALF)], done.at[s, pl.ds(h * HALF, HALF)], fin_send.at[2 * s, h]).wait()
 
 
 def project(theta, gate, vectors, slot_sector, block_offsets, kept):
@@ -344,13 +360,13 @@
         in_specs=[hbm, vmem, hbm, smem, smem, smem],
         out_specs=(vmem, vmem, vmem),
         scratch_shapes=[
-            pltpu.VMEM((16, 2, SHARE, KEPT), bf),
-            pltpu.VMEM((16, 2, SHARE, KEPT), bf),
-            pltpu.VMEM((16, 8, LANES), jnp.float32),
+            pltpu.VMEM((2, 16, SHARE, KEPT), bf),
+            pltpu.VMEM((2, 16, SHARE, KEPT), bf),
+            pltpu.VMEM((2, 16, 8, LANES), jnp.float32),
             pltpu.VMEM((2, SITES * HALF, KEPT), bf),
-            pltpu.VMEM((16, 2, SHARE, KEPT), bf),
-            pltpu.VMEM((16, 2, SHARE, KEPT), bf),
-            pltpu.VMEM((16, 8, LANES), jnp.float32),
+            pltpu.VMEM((2, 16, SHARE, KEPT), bf),
+            pltpu.VMEM((2, 16, SHARE, KEPT), bf),
+            pltpu.VMEM((2, 16, 8, LANES), jnp.float32),
             pltpu.VMEM((ROWS + NMAX, 16, LANES), bf),
             pltpu.VMEM((256, 256), bf),
             pltpu.VMEM((SITES * NMAX, KEPT), bf),
@@ -364,7 +380,7 @@
             dma, dma, dma((14,)), dma((8, 2)),
             dma((UNITS, 2)), dma((UNITS, 2)), dma((UNITS, 2)), dma((UNITS, 2)),
             dma((UNITS, 3)), dma((UNITS, 3)), dma((UNITS, 2)), dma((2, 16)),
-        ] + [dma((16,))] * 10,
+        ] + [dma((2, 16))] * 10,
         compiler_params=pltpu.CompilerParams(has_side_effects=True, collective_id=0, vmem_limit_bytes=56 * 2**20),
         cost_estimate=pl.CostEstimate(flops=5_000_000_000, bytes_accessed=6_000_000, transcendentals=0),
         name="project",

time: 127 us -> 119 us (0.937)
  the two profiles are of different devices: /device:TPU:86 before, /device:TPU:1 now
where the time goes in v5:
time: 119 us
  Pallas kernels  109 us (92%)
  local copies, waits for them, and re-layouts  5.01 us (4%)
  matrix products  3.63 us (3%)
    pallas_call x1, Pallas kernels, project(): pl.pallas_call(project_kernel, out_shape=(jax.ShapeDtypeStruct((2, SITES,...  109 us

profile of v5, /device:TPU:1, one launch (start us, length us, event | category | flops | bytes accessed | tf_op | source)
XLA Modules:
  0.0 118.8 jit_solution(4317009378933516823)
XLA Ops:
  0.6 1.4 %reshape.26.gate_ref = bf16[16,16]{1,0:T(8,128)(2,1)} reshape(bf16[4,4,4,4]{3,2,1,0:T(4,128)(2,1)} %param.7) | data formatting | bytes 1024 | tf_op jit(solution)/shard_map/reshape | solution.py:393
  2.0 109.4 %project.1 = (bf16[2,4,4,48,128]{4,3,2,1,0:T(8,128)(2,1)}, bf16[2,16,32,512]{3,2,1,0:T(8,128)(2,1)}, f32[2,8,512]{2,1,0:T(8,128)}) custom-call(bf16[1024,16,128]{2,1,0:T(8,128)(2,1)} %bitcast.30, bf16[16,16]{1,0:T(8,128)(2,1)} %reshape.26.gate_ref, bf16[2,512,512]{2,1,0:T(8,128)(2,1)} %bitcast.24, s32[16]{0:T(128)} %sector_ref.1, s32[8,16]{1,0:T(8,128)} %offset_ref.1, ...), custom_call_target="tpu_custom_call" | custom-call | flops 5000000000 | bytes 6000000 | tf_op jit(solution)/shard_map/project/pallas_call | solution.py:353
  111.5 1.2 copy.9
  112.6 0.2 reshape.28
  112.8 0.0 copy-start
  112.8 0.0 copy-start.1
  112.8 0.9 slice.3
  113.7 1.6 %fusion.1 = f32[2,192,512]{2,1,0:T(8,128)S(1)} fusion(bf16[2,192,512]{2,1,0:T(8,128)(2,1)S(1)} %reshape.28, bf16[2,512,512]{2,1,0:T(8,128)(2,1)} %bitcast.20, f32[2,512]{1,0:T(2,128)S(1)} %bitcast.28), kind=kOutput, calls=%fused_computation.3 | convolution fusion | flops 201916416 | bytes 2232320 | tf_op jit(solution)/shard_map/snk,skl->snl/dot_general | solution.py:402
  115.3 1.4 %copy.14 = f32[2,4,48,512]{3,1,0,2:T(4,128)} copy(f32[2,4,48,512]{3,2,1,0:T(8,128)S(1)} %bitcast.22) | data formatting | bytes 1572864 | tf_op jit(solution)/shard_map/reshape | solution.py:406
  116.7 0.0 copy-done
  116.7 0.0 copy-done.1
  116.7 2.0 %fusion = f32[2,512,512]{2,1,0:T(8,128)} fusion(bf16[2,512,512]{2,1,0:T(8,128)(2,1)S(1)} %bitcast.25, bf16[2,512,512]{2,1,0:T(8,128)(2,1)S(1)} %bitcast.21, f32[2,512]{1,0:T(2,128)S(1)} %bitcast.29), kind=kOutput, calls=%fused_computation.1 | convolution fusion | flops 538443776 | bytes 4198400 | tf_op jit(solution)/shard_map/snk,skl->snl/dot_general | solution.py:398
  (1 shorter events, 0.0 us)
Async XLA Ops:
  112.8 3.9 %copy-start = (bf16[2,16,32,512]{3,2,1,0:T(8,128)(2,1)S(1)}, bf16[2,16,32,512]{3,2,1,0:T(8,128)(2,1)}, u32[]{:S(2)}) copy-start(bf16[2,16,32,512]{3,2,1,0:T(8,128)(2,1)} %get-tuple-element.6) | copy-start | bytes 3145732
  112.8 3.9 %copy-start.1 = (bf16[2,4,128,512]{3,2,1,0:T(8,128)(2,1)S(1)}, bf16[2,4,128,512]{3,2,1,0:T(8,128)(2,1)}, u32[]{:S(2)}) copy-start(bf16[2,4,128,512]{3,2,1,0:T(8,128)(2,1)} %param.8) | copy-start | bytes 3145732

commit v6 on v5

--- a/solution.py
+++ b/solution.py
@@ -82,7 +82,7 @@
 
 
 def project_kernel(
-    theta_ref, gate_ref, v_ref, sector_ref, offset_ref, kept_ref, fin_ref, out_ref, mask_ref,
+    theta_ref, gate_ref, v_ref, sector_ref, offset_ref, kept_ref, fin_ref, out_ref,
     corr_out, corr_in, corr_diag_in, factor, gram_out, gram_in, gram_diag_in, th, bd, ap, vall, part, half_in, ring_in, quart, quart_in, done,
     th_sem, v_sem, v_send, v_recv, half_send, half_recv, ring_send, ring_recv,
     quart_send, quart_recv, fin_send, fin_recv, corr_send, corr_recv, corr_diag_send, corr_diag_recv,
@@ -147,13 +147,16 @@
     v_in = pltpu.make_async_copy(v_ref, vall.at[0], v_sem)
     v_in.start()
 
-    big_r = lax.broadcasted_iota(jnp.int32, (256, 256), 0)
-    big_c = lax.broadcasted_iota(jnp.int32, (256, 256), 1)
-    left_hot = (lax.broadcasted_iota(jnp.int32, (256, 16), 0) // 16 == lax.broadcasted_iota(jnp.int32, (256, 16), 1))
-    right_hot = (lax.broadcasted_iota(jnp.int32, (16, 256), 1) % 16 == lax.broadcasted_iota(jnp.int32, (16, 256), 0))
-    spread = jnp.dot(left_hot.astype(jnp.bfloat16), gate_ref[...], preferred_element_type=jnp.float32)
-    spread = jnp.dot(spread.astype(jnp.bfloat16), right_hot.astype(jnp.bfloat16), preferred_element_type=jnp.float32)
-    bd[...] = jnp.where(big_r % 16 == big_c // 16, spread, 0.0).astype(jnp.bfloat16)
+    pair_r = lax.broadcasted_iota(jnp.int32, (4, 256), 0)
+    pair_c = lax.broadcasted_iota(jnp.int32, (4, 256), 1)
+    second_in = (pair_r == pair_c % 4).astype(jnp.bfloat16)
+    same = lax.broadcasted_iota(jnp.int32, (16, 256), 0) == lax.broadcasted_iota(jnp.int32, (16, 256), 1) // 16
+    for a in range(4):
+        for b in range(4):
+            spread = jnp.dot(gate_ref[a, b], second_in, preferred_element_type=jnp.float32)
+            spread = jnp.sum(jnp.where(pair_r == pair_c // 4 % 4, spread, 0.0), axis=0, keepdims=True)
+            spread = jnp.where(same, jnp.broadcast_to(spread, (16, 256)), 0.0)
+            bd[(a * 4 + b) * 16:(a * 4 + b + 1) * 16] = spread.astype(jnp.bfloat16)
     th[pl.ds(ROWS, NMAX)] = jnp.zeros((NMAX, 16, LANES), jnp.bfloat16)
     pl.semaphore_wait(barrier, jnp.where(home, 33, 34))
 
@@ -301,8 +304,6 @@
         result = jnp.where(at_row == at_col, 0.5 * (1.0 - norms), offdiag)
         result = jnp.where((at_row < kept) & (at_col < kept), result, 0.0)
         out_ref[s, col] = result.astype(jnp.bfloat16)
-        lanes = lax.broadcasted_iota(jnp.int32, (8, KEPT), 1)
-        mask_ref[s] = jnp.where(lanes < kept, 1.0, 0.0)
         start_shared(out_ref.at[s], out_send.at[s], out_recv.at[s], row, col)
 
     each(compute, 0)
@@ -355,10 +356,9 @@
         out_shape=(
             jax.ShapeDtypeStruct((2, SITES, 4, HALF, LANES), bf),
             jax.ShapeDtypeStruct((2, 16, SHARE, KEPT), bf),
-            jax.ShapeDtypeStruct((2, 8, KEPT), jnp.float32),
         ),
         in_specs=[hbm, vmem, hbm, smem, smem, smem],
-        out_specs=(vmem, vmem, vmem),
+        out_specs=(vmem, vmem),
         scratch_shapes=[
             pltpu.VMEM((2, 16, SHARE, KEPT), bf),
             pltpu.VMEM((2, 16, SHARE, KEPT), bf),
@@ -387,24 +387,54 @@
     )(theta, gate, vectors, slot_sector, block_offsets, kept)
 
 
+def final_kernel(sector_ref, kept_ref, v_ref, corr_ref, fin_ref, left_ref, right_ref):
+    s = pl.program_id(0)
+    kept = kept_ref[sector_ref[2 * lax.axis_index("row") + s]]
+    corr_b = corr_ref[0].reshape(KEPT, KEPT)
+
+    def keep(values):
+        return jnp.where(lax.broadcasted_iota(jnp.int32, values.shape, 1) < kept, values, 0.0)
+
+    for n in range(0, KEPT, 256):
+        block = v_ref[0, n:n + 256]
+        change = jnp.dot(block, corr_b, preferred_element_type=jnp.float32)
+        right_ref[0, n:n + 256] = keep(block.astype(jnp.float32) + change)
+    for a in range(SITES):
+        block = jnp.concatenate([fin_ref[0, a, q] for q in range(4)], axis=1)
+        change = jnp.dot(block, corr_b, preferred_element_type=jnp.float32)
+        left_ref[:, 0, a, :] = keep(block.astype(jnp.float32) + change)
+
+
+def final(slot_sector, kept, vectors, corr_b, fin):
+    smem = pl.BlockSpec(memory_space=pltpu.SMEM)
+    return pl.pallas_call(
+        final_kernel,
+        grid=(2,),
+        out_shape=(
+            jax.ShapeDtypeStruct((HALF, 2, SITES, KEPT), jnp.float32),
+            jax.ShapeDtypeStruct((2, KEPT, KEPT), jnp.float32),
+        ),
+        in_specs=[
+            smem, smem,
+            pl.BlockSpec((1, KEPT, KEPT), lambda s: (s, 0, 0)),
+            pl.BlockSpec((1, 16, SHARE, KEPT), lambda s: (s, 0, 0, 0)),
+            pl.BlockSpec((1, SITES, 4, HALF, LANES), lambda s: (s, 0, 0, 0, 0)),
+        ],
+        out_specs=(
+            pl.BlockSpec((HALF, 1, SITES, KEPT), lambda s: (0, s, 0, 0)),
+            pl.BlockSpec((1, KEPT, KEPT), lambda s: (s, 0, 0)),
+        ),
+        compiler_params=pltpu.CompilerParams(vmem_limit_bytes=32 * 2**20),
+        cost_estimate=pl.CostEstimate(flops=800_000_000, bytes_accessed=5_500_000, transcendentals=0),
+        name="final",
+    )(slot_sector, kept, vectors, corr_b, fin)
+
+
 def shards(theta, gate, warm_start, slot_sector, kept, block_offsets):
     vectors = warm_start.reshape(2, KEPT, KEPT)
-    fin, corr_b, mask = project(
-        theta.reshape(ROWS, 16, LANES), gate.reshape(16, 16), vectors, slot_sector, block_offsets, kept
-    )
-    corr_b = corr_b.reshape(2, KEPT, KEPT)
-    kept_mask = mask[:, 0]
-    projected_b = fin.transpose(0, 1, 3, 2, 4).reshape(2, SITES * HALF, KEPT)
-    new_vectors = vectors.astype(jnp.float32) + jnp.einsum(
-        "snk,skl->snl", vectors, corr_b, preferred_element_type=jnp.float32
-    )
-    new_vectors = new_vectors * kept_mask[:, None, :]
-    left = projected_b.astype(jnp.float32) + jnp.einsum(
-        "snk,skl->snl", projected_b, corr_b, preferred_element_type=jnp.float32
-    )
-    left = left * kept_mask[:, None, :]
-    left = left.reshape(2, SITES, HALF, KEPT).transpose(2, 0, 1, 3)
-    return (left, new_vectors.reshape(2, 4, LANES, KEPT))
+    fin, corr_b = project(theta.reshape(ROWS, 16, LANES), gate, vectors, slot_sector, block_offsets, kept)
+    left, right = final(slot_sector, kept, vectors, corr_b, fin)
+    return left, right.reshape(2, 4, LANES, KEPT)
 
 
 def solution(mesh):

time: 119 us -> 116 us (0.975)
  Pallas kernels: 109 us -> 113 us
  matrix products: 3.63 us -> 0 us
  local copies, waits for them, and re-layouts: 5.01 us -> 2.23 us
    dot_general x2 -> x0, matrix products: 3.63 us -> none  [the longest x1 2.03 us: shards(): jnp.einsum('snk,skl->snl', vectors, corr_b, preferred_element_type=jnp.fl...]
    pallas_call x0 -> x1, Pallas kernels: none -> 3.07 us  [final(): pl.pallas_call(final_kernel, grid=(2,), out_shape=(jax.ShapeDtypeStruct((...]
    reshape x3 -> x0, local copies, waits for them, and re-layouts: 2.94 us -> none  [the longest x1 1.4 us: shards(): gate.reshape(16, 16)]
    unnamed x5 -> x10, local copies, waits for them, and re-layouts: 0.02 us -> 2.23 us
where the time goes in v6:
time: 116 us; the launch traced here: 115 us
  Pallas kernels  113 us (97%)
  local copies, waits for them, and re-layouts  2.23 us (2%)
    pallas_call x1, Pallas kernels, project(): pl.pallas_call(project_kernel, out_shape=(jax.ShapeDtypeStruct((2, SITES,...  109 us
    pallas_call x1, Pallas kernels, final(): pl.pallas_call(final_kernel, grid=(2,), out_shape=(jax.ShapeDtypeStruct((...  3.07 us

profile of v6, /device:TPU:1, one launch (start us, length us, event | category | flops | bytes accessed | tf_op | source)
XLA Modules:
  0.0 115.5 jit_solution(10131923701660233551)
XLA Ops:
  0.6 0.0 copy-start
  0.6 0.0 copy-start.1
  0.7 0.0 copy-start.2
  0.7 109.5 %project.1 = (bf16[2,4,4,48,128]{4,3,2,1,0:T(8,128)(2,1)}, bf16[2,16,32,512]{3,2,1,0:T(8,128)(2,1)}) custom-call(bf16[1024,16,128]{2,1,0:T(8,128)(2,1)} %bitcast.5, bf16[4,4,4,4]{3,2,1,0:T(4,128)(2,1)} %gate_ref.1, bf16[2,512,512]{2,1,0:T(8,128)(2,1)} %bitcast.3, s32[16]{0:T(128)} %sector_ref.3, s32[8,16]{1,0:T(8,128)} %offset_ref.1, s32[16]{0:T(128)} %kept_ref.3), custom_call_target="tpu_custom_call" | custom-call | flops 5000000000 | bytes 6000000 | tf_op jit(solution)/shard_map/project/pallas_call | solution.py:354
  110.2 0.0 copy-done
  110.2 0.0 copy-done.1
  110.2 0.0 copy-done.2
  110.2 0.0 copy-start.3
  110.2 1.2 %copy-done.3 = bf16[2,16,32,512]{3,2,1,0:T(8,128)(2,1)S(1)} copy-done((bf16[2,16,32,512]{3,2,1,0:T(8,128)(2,1)S(1)}, bf16[2,16,32,512]{3,2,1,0:T(8,128)(2,1)}, u32[]{:S(2)}) %copy-start.3) | copy-done | bytes 1048600
  111.4 0.0 copy-start.4
  111.4 1.0 copy-done.4
  112.4 3.1 %final.1 = (f32[48,2,4,512]{3,2,1,0:T(4,128)}, f32[2,512,512]{2,1,0:T(8,128)}) custom-call(s32[16]{0:T(128)S(1)} %copy-done.1, s32[16]{0:T(128)S(1)} %copy-done.2, bf16[2,512,512]{2,1,0:T(8,128)(2,1)S(1)} %bitcast.4, bf16[2,16,32,512]{3,2,1,0:T(8,128)(2,1)S(1)} %copy-done.3, bf16[2,4,4,48,128]{4,3,2,1,0:T(8,128)(2,1)S(1)} %copy-done.4), custom_call_target="tpu_custom_call" | custom-call | flops 800000000 | bytes 5500000 | tf_op jit(solution)/shard_map/final/pallas_call | solution.py:410
Async XLA Ops:
  0.6 109.5 %copy-start = (bf16[2,4,128,512]{3,2,1,0:T(8,128)(2,1)S(1)}, bf16[2,4,128,512]{3,2,1,0:T(8,128)(2,1)}, u32[]{:S(2)}) copy-start(bf16[2,4,128,512]{3,2,1,0:T(8,128)(2,1)} %param.8) | copy-start | bytes 3145732
  0.6 109.5 %copy-start.1 = (s32[16]{0:T(128)S(1)}, s32[16]{0:T(128)}, u32[]{:S(2)}) copy-start(s32[16]{0:T(128)} %sector_ref.3) | copy-start | bytes 196
  0.7 109.5 %copy-start.2 = (s32[16]{0:T(128)S(1)}, s32[16]{0:T(128)}, u32[]{:S(2)}) copy-start(s32[16]{0:T(128)} %kept_ref.3) | copy-start | bytes 196
  110.2 1.2 %copy-start.3 = (bf16[2,16,32,512]{3,2,1,0:T(8,128)(2,1)S(1)}, bf16[2,16,32,512]{3,2,1,0:T(8,128)(2,1)}, u32[]{:S(2)}) copy-start(bf16[2,16,32,512]{3,2,1,0:T(8,128)(2,1)} %get-tuple-element.6.corr_ref) | copy-start | bytes 3145732
  111.4 1.0 copy-start.4

commit v7 on v6

--- a/solution.py
+++ b/solution.py
@@ -24,7 +24,7 @@
 UNITS = len(ORDER)
 
 
-def overlap(block, out, diag, col):
+def overlap(block, out, diag, first, col):
     product = lax.dot_general(block, block, (((0,), (0,)), ((), ())), preferred_element_type=jnp.float32)
     product = product.astype(jnp.bfloat16)
     for c in range(16):
@@ -32,7 +32,7 @@
     wide = block.astype(jnp.float32)
     squares = jnp.sum(wide * wide, axis=0, keepdims=True)
     for q in range(4):
-        diag[col, q:q + 1] = squares[:, q * LANES:(q + 1) * LANES]
+        diag[col, first + q:first + q + 1] = squares[:, q * LANES:(q + 1) * LANES]
 
 
 def start_exchange(out, into, send_sem, recv_sem, row, col):
@@ -83,10 +83,10 @@
 
 def project_kernel(
     theta_ref, gate_ref, v_ref, sector_ref, offset_ref, kept_ref, fin_ref, out_ref,
-    corr_out, corr_in, corr_diag_in, factor, gram_out, gram_in, gram_diag_in, th, bd, ap, vall, part, half_in, ring_in, quart, quart_in, done,
+    corr_out, corr_in, factor, gram_out, gram_in, diag_in, th, bd, ap, vall, part, half_in, ring_in, quart, quart_in, done,
     th_sem, v_sem, v_send, v_recv, half_send, half_recv, ring_send, ring_recv,
-    quart_send, quart_recv, fin_send, fin_recv, corr_send, corr_recv, corr_diag_send, corr_diag_recv,
-    gram_send, gram_recv, gram_diag_send, gram_diag_recv, out_send, out_recv,
+    quart_send, quart_recv, fin_send, fin_recv, corr_send, corr_recv,
+    gram_send, gram_recv, diag_send, diag_recv, out_send, out_recv,
 ):
     row, col = lax.axis_index("row"), lax.axis_index("col")
     x, core = row // 2, row % 2
@@ -270,8 +270,7 @@
 
     def start_corr():
         for s in range(2):
-            overlap(vall[0, s], corr_out.at[s], corr_diag_in.at[s], col)
-            start_shared(corr_diag_in.at[s], corr_diag_send.at[s], corr_diag_recv.at[s], row, col)
+            overlap(vall[0, s], corr_out.at[s], diag_in.at[s], 4, col)
             start_exchange(corr_out.at[s], corr_in.at[s], corr_send.at[s], corr_recv.at[s], row, col)
 
     def start_gram(s):
@@ -282,15 +281,15 @@
         for a in range(SITES):
             for q in range(4):
                 factor[s, a * HALF:(a + 1) * HALF, q * LANES:(q + 1) * LANES] = fin_ref[s, a, q]
-        overlap(factor[s], gram_out.at[s], gram_diag_in.at[s], col)
-        start_shared(gram_diag_in.at[s], gram_diag_send.at[s], gram_diag_recv.at[s], row, col)
+        overlap(factor[s], gram_out.at[s], diag_in.at[s], 0, col)
+        start_shared(diag_in.at[s], diag_send.at[s], diag_recv.at[s], row, col)
         start_exchange(gram_out.at[s], gram_in.at[s], gram_send.at[s], gram_recv.at[s], row, col)
 
     def refine(s):
         correlation = finish_exchange(corr_out.at[s], corr_in.at[s], corr_send.at[s], corr_recv.at[s], col)
-        corr_diag = finish_shared(corr_diag_in.at[s], corr_diag_send.at[s], corr_diag_recv.at[s], col)
-        gram_diag = finish_shared(gram_diag_in.at[s], gram_diag_send.at[s], gram_diag_recv.at[s], col)
-        lambdas = gram_diag / (corr_diag + 1e-06)
+        diags = finish_shared(diag_in.at[s], diag_send.at[s], diag_recv.at[s], col)
+        corr_diag = diags[4:]
+        lambdas = diags[:4] / (corr_diag + 1e-06)
         gram = finish_exchange(gram_out.at[s], gram_in.at[s], gram_send.at[s], gram_recv.at[s], col)
         kept = kept_ref[sector_ref[2 * row + s]]
         across = jnp.concatenate([lambdas[q:q + 1] for q in range(4)], axis=1)
@@ -362,7 +361,6 @@
         scratch_shapes=[
             pltpu.VMEM((2, 16, SHARE, KEPT), bf),
             pltpu.VMEM((2, 16, SHARE, KEPT), bf),
-            pltpu.VMEM((2, 16, 8, LANES), jnp.float32),
             pltpu.VMEM((2, SITES * HALF, KEPT), bf),
             pltpu.VMEM((2, 16, SHARE, KEPT), bf),
             pltpu.VMEM((2, 16, SHARE, KEPT), bf),
@@ -380,7 +378,7 @@
             dma, dma, dma((14,)), dma((8, 2)),
             dma((UNITS, 2)), dma((UNITS, 2)), dma((UNITS, 2)), dma((UNITS, 2)),
             dma((UNITS, 3)), dma((UNITS, 3)), dma((UNITS, 2)), dma((2, 16)),
-        ] + [dma((2, 16))] * 10,
+        ] + [dma((2, 16))] * 8,
         compiler_params=pltpu.CompilerParams(has_side_effects=True, collective_id=0, vmem_limit_bytes=56 * 2**20),
         cost_estimate=pl.CostEstimate(flops=5_000_000_000, bytes_accessed=6_000_000, transcendentals=0),
         name="project",

time: 116 us -> 114 us (0.983)
  Pallas kernels: 113 us -> 111 us
where the time goes in v7:
time: 114 us
  Pallas kernels  111 us (97%)
  local copies, waits for them, and re-layouts  2.23 us (2%)
    pallas_call x1, Pallas kernels, project(): pl.pallas_call(project_kernel, out_shape=(jax.ShapeDtypeStruct((2, SITES,...  108 us
    pallas_call x1, Pallas kernels, final(): pl.pallas_call(final_kernel, grid=(2,), out_shape=(jax.ShapeDtypeStruct((...  3.07 us

profile of v7, /device:TPU:1, one launch (start us, length us, event | category | flops | bytes accessed | tf_op | source)
XLA Modules:
  0.0 114.3 jit_solution(8559072649592196607)
XLA Ops:
  0.6 0.0 copy-start
  0.6 0.0 copy-start.1
  0.7 0.0 copy-start.2
  0.7 108.3 %project.1 = (bf16[2,4,4,48,128]{4,3,2,1,0:T(8,128)(2,1)}, bf16[2,16,32,512]{3,2,1,0:T(8,128)(2,1)}) custom-call(bf16[1024,16,128]{2,1,0:T(8,128)(2,1)} %bitcast.5, bf16[4,4,4,4]{3,2,1,0:T(4,128)(2,1)} %gate_ref.1, bf16[2,512,512]{2,1,0:T(8,128)(2,1)} %bitcast.3, s32[16]{0:T(128)} %sector_ref.3, s32[8,16]{1,0:T(8,128)} %offset_ref.1, s32[16]{0:T(128)} %kept_ref.3), custom_call_target="tpu_custom_call" | custom-call | flops 5000000000 | bytes 6000000 | tf_op jit(solution)/shard_map/project/pallas_call | solution.py:353
  109.0 0.0 copy-done
  109.0 0.0 copy-done.1
  109.0 0.0 copy-done.2
  109.0 0.0 copy-start.3
  109.0 1.2 %copy-done.3 = bf16[2,16,32,512]{3,2,1,0:T(8,128)(2,1)S(1)} copy-done((bf16[2,16,32,512]{3,2,1,0:T(8,128)(2,1)S(1)}, bf16[2,16,32,512]{3,2,1,0:T(8,128)(2,1)}, u32[]{:S(2)}) %copy-start.3) | copy-done | bytes 1048600
  110.3 0.0 copy-start.4
  110.3 1.0 copy-done.4
  111.3 3.1 %final.1 = (f32[48,2,4,512]{3,2,1,0:T(4,128)}, f32[2,512,512]{2,1,0:T(8,128)}) custom-call(s32[16]{0:T(128)S(1)} %copy-done.1, s32[16]{0:T(128)S(1)} %copy-done.2, bf16[2,512,512]{2,1,0:T(8,128)(2,1)S(1)} %bitcast.4, bf16[2,16,32,512]{3,2,1,0:T(8,128)(2,1)S(1)} %copy-done.3, bf16[2,4,4,48,128]{4,3,2,1,0:T(8,128)(2,1)S(1)} %copy-done.4), custom_call_target="tpu_custom_call" | custom-call | flops 800000000 | bytes 5500000 | tf_op jit(solution)/shard_map/final/pallas_call | solution.py:408
Async XLA Ops:
  0.6 108.4 %copy-start = (bf16[2,4,128,512]{3,2,1,0:T(8,128)(2,1)S(1)}, bf16[2,4,128,512]{3,2,1,0:T(8,128)(2,1)}, u32[]{:S(2)}) copy-start(bf16[2,4,128,512]{3,2,1,0:T(8,128)(2,1)} %param.8) | copy-start | bytes 3145732
  0.6 108.4 %copy-start.1 = (s32[16]{0:T(128)S(1)}, s32[16]{0:T(128)}, u32[]{:S(2)}) copy-start(s32[16]{0:T(128)} %sector_ref.3) | copy-start | bytes 196
  0.7 108.4 %copy-start.2 = (s32[16]{0:T(128)S(1)}, s32[16]{0:T(128)}, u32[]{:S(2)}) copy-start(s32[16]{0:T(128)} %kept_ref.3) | copy-start | bytes 196
  109.0 1.2 %copy-start.3 = (bf16[2,16,32,512]{3,2,1,0:T(8,128)(2,1)S(1)}, bf16[2,16,32,512]{3,2,1,0:T(8,128)(2,1)}, u32[]{:S(2)}) copy-start(bf16[2,16,32,512]{3,2,1,0:T(8,128)(2,1)} %get-tuple-element.6.corr_ref) | copy-start | bytes 3145732
  110.3 1.0 copy-start.4

commit v8 on v7

--- a/solution.py
+++ b/solution.py
@@ -62,7 +62,6 @@
     def _(d):
         source = (col + d) % 16
         wait_on(into.at[source], recv_sem.at[source])
-        wait_on(out.at[source], send_sem.at[source])
 
     into[col] = out[col]
     total = into[0].astype(jnp.float32)
@@ -76,7 +75,6 @@
     def _(d):
         source = (col + d) % 16
         wait_on(both.at[source], recv_sem.at[source])
-        wait_on(both.at[col], send_sem.at[source])
 
     return jnp.sum(both[...], axis=0)
 
@@ -331,9 +329,10 @@
     for s in range(2):
         @pl.loop(1, 16)
         def _(d):
-            source = (col + d) % 16
-            wait_on(out_ref.at[s, source], out_recv.at[s, source])
-            wait_on(out_ref.at[s, col], out_send.at[s, source])
+            to = (col + d) % 16
+            wait_on(corr_out.at[s, to], corr_send.at[s, to])
+            wait_on(gram_out.at[s, to], gram_send.at[s, to])
+            wait_on(diag_in.at[s, col], diag_send.at[s, to])
 
     for copy in sends:
         copy.wait_send()
@@ -342,6 +341,13 @@
             @pl.when(col != 2 * row + h)
             def _():
                 pltpu.make_async_copy(done.at[s, pl.ds(h * HALF, HALF)], done.at[s, pl.ds(h * HALF, HALF)], fin_send.at[2 * s, h]).wait()
+
+    for s in range(2):
+        @pl.loop(1, 16)
+        def _(d):
+            source = (col + d) % 16
+            wait_on(out_ref.at[s, source], out_recv.at[s, source])
+            wait_on(out_ref.at[s, col], out_send.at[s, source])
 
 
 def project(theta, gate, vectors, slot_sector, block_offsets, kept):

time: 114 us -> 115 us (level); the launches traced: 114 us -> 114 us
  no operation moved by 1% of the time
where the time goes in v8:
time: 115 us; the launch traced here: 114 us
  Pallas kernels  111 us (97%)
  local copies, waits for them, and re-layouts  2.23 us (2%)
    pallas_call x1, Pallas kernels, project(): pl.pallas_call(project_kernel, out_shape=(jax.ShapeDtypeStruct((2, SITES,...  108 us
    pallas_call x1, Pallas kernels, final(): pl.pallas_call(final_kernel, grid=(2,), out_shape=(jax.ShapeDtypeStruct((...  3.07 us

profile of v8, /device:TPU:1, one launch (start us, length us, event | category | flops | bytes accessed | tf_op | source)
XLA Modules:
  0.0 114.1 jit_solution(2415944663206060515)
XLA Ops:
  0.6 0.0 copy-start
  0.6 0.0 copy-start.1
  0.7 0.0 copy-start.2
  0.7 108.1 %project.1 = (bf16[2,4,4,48,128]{4,3,2,1,0:T(8,128)(2,1)}, bf16[2,16,32,512]{3,2,1,0:T(8,128)(2,1)}) custom-call(bf16[1024,16,128]{2,1,0:T(8,128)(2,1)} %bitcast.5, bf16[4,4,4,4]{3,2,1,0:T(4,128)(2,1)} %gate_ref.1, bf16[2,512,512]{2,1,0:T(8,128)(2,1)} %bitcast.3, s32[16]{0:T(128)} %sector_ref.3, s32[8,16]{1,0:T(8,128)} %offset_ref.1, s32[16]{0:T(128)} %kept_ref.3), custom_call_target="tpu_custom_call" | custom-call | flops 5000000000 | bytes 6000000 | tf_op jit(solution)/shard_map/project/pallas_call | solution.py:359
  108.7 0.0 copy-done
  108.7 0.0 copy-done.1
  108.8 0.0 copy-done.2
  108.8 0.0 copy-start.3
  108.8 1.2 %copy-done.3 = bf16[2,16,32,512]{3,2,1,0:T(8,128)(2,1)S(1)} copy-done((bf16[2,16,32,512]{3,2,1,0:T(8,128)(2,1)S(1)}, bf16[2,16,32,512]{3,2,1,0:T(8,128)(2,1)}, u32[]{:S(2)}) %copy-start.3) | copy-done | bytes 1048600
  110.0 0.0 copy-start.4
  110.0 1.0 copy-done.4
  111.0 3.1 %final.1 = (f32[48,2,4,512]{3,2,1,0:T(4,128)}, f32[2,512,512]{2,1,0:T(8,128)}) custom-call(s32[16]{0:T(128)S(1)} %copy-done.1, s32[16]{0:T(128)S(1)} %copy-done.2, bf16[2,512,512]{2,1,0:T(8,128)(2,1)S(1)} %bitcast.4, bf16[2,16,32,512]{3,2,1,0:T(8,128)(2,1)S(1)} %copy-done.3, bf16[2,4,4,48,128]{4,3,2,1,0:T(8,128)(2,1)S(1)} %copy-done.4), custom_call_target="tpu_custom_call" | custom-call | flops 800000000 | bytes 5500000 | tf_op jit(solution)/shard_map/final/pallas_call | solution.py:414
Async XLA Ops:
  0.6 108.1 %copy-start = (bf16[2,4,128,512]{3,2,1,0:T(8,128)(2,1)S(1)}, bf16[2,4,128,512]{3,2,1,0:T(8,128)(2,1)}, u32[]{:S(2)}) copy-start(bf16[2,4,128,512]{3,2,1,0:T(8,128)(2,1)} %param.8) | copy-start | bytes 3145732
  0.6 108.1 %copy-start.1 = (s32[16]{0:T(128)S(1)}, s32[16]{0:T(128)}, u32[]{:S(2)}) copy-start(s32[16]{0:T(128)} %sector_ref.3) | copy-start | bytes 196
  0.7 108.1 %copy-start.2 = (s32[16]{0:T(128)S(1)}, s32[16]{0:T(128)}, u32[]{:S(2)}) copy-start(s32[16]{0:T(128)} %kept_ref.3) | copy-start | bytes 196
  108.8 1.2 %copy-start.3 = (bf16[2,16,32,512]{3,2,1,0:T(8,128)(2,1)S(1)}, bf16[2,16,32,512]{3,2,1,0:T(8,128)(2,1)}, u32[]{:S(2)}) copy-start(bf16[2,16,32,512]{3,2,1,0:T(8,128)(2,1)} %get-tuple-element.6.corr_ref) | copy-start | bytes 3145732
  110.0 1.0 copy-start.4

commit v9 on v7

--- a/solution.py
+++ b/solution.py
@@ -158,6 +158,9 @@
             spread = jnp.where(same, jnp.broadcast_to(spread, (16, 256)), 0.0)
             bd[(a * 4 + b) * 16:(a * 4 + b + 1) * 16] = spread.astype(jnp.bfloat16)
     th[pl.ds(ROWS, NMAX)] = jnp.zeros((NMAX, 16, LANES), jnp.bfloat16)
+    v_in.wait()
+    for s in range(2):
+        overlap(vall[0, s], corr_out.at[s], diag_in.at[s], 4, col)
     pl.semaphore_wait(barrier, jnp.where(home, 33, 34))
 
     def send_own(s, n):
@@ -167,7 +170,6 @@
     for s, n in ((0, 2), (0, 0), (0, 1), (1, 2)):
         send_own(s, n)
     theta_in.wait()
-    v_in.wait()
 
     state = lax.broadcasted_iota(jnp.int32, (256, 256), 0) % 16
     state = state + 16 * (lax.broadcasted_iota(jnp.int32, (256, 256), 1) // LANES)
@@ -270,7 +272,6 @@
 
     def start_corr():
         for s in range(2):
-            overlap(vall[0, s], corr_out.at[s], diag_in.at[s], 4, col)
             start_exchange(corr_out.at[s], corr_in.at[s], corr_send.at[s], corr_recv.at[s], row, col)
 
     def start_gram(s):

time: 114 us -> 115 us (level)
  no operation moved by 1% of the time
where the time goes in v9:
time: 115 us
  Pallas kernels  112 us (97%)
  local copies, waits for them, and re-layouts  2.23 us (2%)
    pallas_call x1, Pallas kernels, project(): pl.pallas_call(project_kernel, out_shape=(jax.ShapeDtypeStruct((2, SITES,...  109 us
    pallas_call x1, Pallas kernels, final(): pl.pallas_call(final_kernel, grid=(2,), out_shape=(jax.ShapeDtypeStruct((...  3.07 us

profile of v9, /device:TPU:1, one launch (start us, length us, event | category | flops | bytes accessed | tf_op | source)
XLA Modules:
  0.0 115.0 jit_solution(11251274759925975271)
XLA Ops:
  0.6 0.0 copy-start
  0.6 0.0 copy-start.1
  0.7 0.0 copy-start.2
  0.7 109.0 %project.1 = (bf16[2,4,4,48,128]{4,3,2,1,0:T(8,128)(2,1)}, bf16[2,16,32,512]{3,2,1,0:T(8,128)(2,1)}) custom-call(bf16[1024,16,128]{2,1,0:T(8,128)(2,1)} %bitcast.5, bf16[4,4,4,4]{3,2,1,0:T(4,128)(2,1)} %gate_ref.1, bf16[2,512,512]{2,1,0:T(8,128)(2,1)} %bitcast.3, s32[16]{0:T(128)} %sector_ref.3, s32[8,16]{1,0:T(8,128)} %offset_ref.1, s32[16]{0:T(128)} %kept_ref.3), custom_call_target="tpu_custom_call" | custom-call | flops 5000000000 | bytes 6000000 | tf_op jit(solution)/shard_map/project/pallas_call | solution.py:354
  109.6 0.0 copy-done
  109.6 0.0 copy-done.1
  109.6 0.0 copy-done.2
  109.7 0.0 copy-start.3
  109.7 1.2 %copy-done.3 = bf16[2,16,32,512]{3,2,1,0:T(8,128)(2,1)S(1)} copy-done((bf16[2,16,32,512]{3,2,1,0:T(8,128)(2,1)S(1)}, bf16[2,16,32,512]{3,2,1,0:T(8,128)(2,1)}, u32[]{:S(2)}) %copy-start.3) | copy-done | bytes 1048600
  110.9 0.0 copy-start.4
  110.9 1.0 copy-done.4
  111.9 3.1 %final.1 = (f32[48,2,4,512]{3,2,1,0:T(4,128)}, f32[2,512,512]{2,1,0:T(8,128)}) custom-call(s32[16]{0:T(128)S(1)} %copy-done.1, s32[16]{0:T(128)S(1)} %copy-done.2, bf16[2,512,512]{2,1,0:T(8,128)(2,1)S(1)} %bitcast.4, bf16[2,16,32,512]{3,2,1,0:T(8,128)(2,1)S(1)} %copy-done.3, bf16[2,4,4,48,128]{4,3,2,1,0:T(8,128)(2,1)S(1)} %copy-done.4), custom_call_target="tpu_custom_call" | custom-call | flops 800000000 | bytes 5500000 | tf_op jit(solution)/shard_map/final/pallas_call | solution.py:409
Async XLA Ops:
  0.6 109.0 %copy-start = (bf16[2,4,128,512]{3,2,1,0:T(8,128)(2,1)S(1)}, bf16[2,4,128,512]{3,2,1,0:T(8,128)(2,1)}, u32[]{:S(2)}) copy-start(bf16[2,4,128,512]{3,2,1,0:T(8,128)(2,1)} %param.8) | copy-start | bytes 3145732
  0.6 109.0 %copy-start.1 = (s32[16]{0:T(128)S(1)}, s32[16]{0:T(128)}, u32[]{:S(2)}) copy-start(s32[16]{0:T(128)} %sector_ref.3) | copy-start | bytes 196
  0.7 109.0 %copy-start.2 = (s32[16]{0:T(128)S(1)}, s32[16]{0:T(128)}, u32[]{:S(2)}) copy-start(s32[16]{0:T(128)} %kept_ref.3) | copy-start | bytes 196
  109.7 1.2 %copy-start.3 = (bf16[2,16,32,512]{3,2,1,0:T(8,128)(2,1)S(1)}, bf16[2,16,32,512]{3,2,1,0:T(8,128)(2,1)}, u32[]{:S(2)}) copy-start(bf16[2,16,32,512]{3,2,1,0:T(8,128)(2,1)} %get-tuple-element.6.corr_ref) | copy-start | bytes 3145732
  110.9 1.0 copy-start.4
